TPU v7x, 32 devices: a whole 2x2x4 slice. The times are simulated.
32 devices in a mesh: dp: 8 (over z, x), tensor: 4 (over y, core).
Axes of the slice: x: 2, y: 2, z: 4, core: 2. Of those that a mesh axis runs over, the one named last changes fastest.
Arguments:
- gate_pre: bfloat16 [2048, 12800], P('dp', 'tensor'), may hold values from -6 to 6
- up_pre: bfloat16 [2048, 12800], P('dp', 'tensor'), may hold values from -6 to 6
- down_codes: bfloat16 [12800, 2560], P(('tensor', 'dp')), may hold values from -127 to 127
- down_scales: float32 [12800, 10], P(('tensor', 'dp')), may hold values from 4e-05 to 0.00024
- cotangent: bfloat16 [2048, 2560], P(('dp', 'tensor')), may hold values from -6 to 6
Outputs:
- layer_out: bfloat16 [2048, 2560], P(('dp', 'tensor'))
- gate_grad: bfloat16 [2048, 12800], P('dp', 'tensor')
- up_grad: bfloat16 [2048, 12800], P('dp', 'tensor')
- weight_grad: float32 [12800, 2560], P(('tensor', 'dp'))
All inputs are finite; a program needn't handle non-finite values.
Results may differ from a plain program's by a relative error of at most 0.022.
Values may be sent and summed in bfloat16 or wider, within the bound.
No kernel may reach another device: no remote copies, remote signals or barrier semaphores. Data moves between devices by JAX's collectives and lax.ppermute only.
A program may use at most 192 MiB of HBM per device.

v0:
```python
import jax
import jax.numpy as jnp
from jax import lax
from jax.sharding import PartitionSpec as P


def silu_parts(gate_value):
    sigmoid_gate = jax.nn.sigmoid(gate_value)
    return (gate_value * sigmoid_gate, sigmoid_gate)


def dequantize(code_block, scales):
    row_count, full_width = code_block.shape
    nblocks = scales.shape[1]
    blocks = (
        code_block.astype(jnp.float32).reshape(row_count, nblocks, full_width // nblocks)
        * scales[:, :, None]
    )
    return blocks.reshape(row_count, full_width).astype(jnp.bfloat16)


def quantize_rows(hidden, received, nblocks):
    block_count = 4
    row_span = hidden.shape[1] // block_count
    full_width = received.shape[1]
    stacked = jnp.moveaxis(hidden.reshape(hidden.shape[0], block_count, row_span), 1, 0)

    def one_block(columns):
        partial_value = lax.dot_general(
            columns, received, (((0,), (0,)), ((), ())), preferred_element_type=jnp.float32
        )
        blocks = partial_value.reshape(row_span, nblocks, full_width // nblocks)
        scale_rows = (jnp.max(jnp.abs(blocks), axis=2) + 1e-06) / 127.0
        grad_codes = (blocks / scale_rows[:, :, None]).astype(jnp.bfloat16)
        return (grad_codes.reshape(row_span, full_width), scale_rows)

    grad_codes, scale_rows = lax.map(one_block, stacked)
    return (grad_codes.reshape(-1, full_width), scale_rows.reshape(-1, nblocks))


def body(gate_pre, up_pre, down_codes, down_scales, cotangent):
    group_rows, local_hidden = gate_pre.shape
    full_width = down_codes.shape[1]
    nblocks = down_scales.shape[1]
    gate_value = gate_pre.astype(jnp.float32)
    up_value = up_pre.astype(jnp.float32)
    activated, sigmoid_gate = silu_parts(gate_value)
    hidden = (activated * up_value).astype(jnp.bfloat16)
    codes_whole, scales_whole = (
        lax.all_gather(down_codes, "dp", axis=0, tiled=True),
        lax.all_gather(down_scales.astype(jnp.bfloat16), "dp", axis=0, tiled=True).astype(
            down_scales.dtype
        ),
    )
    weight = dequantize(codes_whole, scales_whole)
    partial_value = jnp.dot(hidden, weight, preferred_element_type=jnp.float32)
    totals = lax.psum(partial_value.astype(jnp.bfloat16), "tensor").astype(jnp.float32)
    own_rows = group_rows // lax.axis_size("tensor")
    mine = lax.dynamic_slice_in_dim(totals, lax.axis_index("tensor") * own_rows, own_rows, 0)
    layer_out = mine.astype(jnp.bfloat16)
    received = lax.all_gather(cotangent, "tensor", axis=0, tiled=True)
    dhidden = lax.dot_general(
        received, weight, (((1,), (1,)), ((), ())), preferred_element_type=jnp.float32
    )
    gate_grad = (
        dhidden * up_value * sigmoid_gate * (1.0 + gate_value * (1.0 - sigmoid_gate))
    ).astype(jnp.bfloat16)
    up_grad = (dhidden * activated).astype(jnp.bfloat16)
    grad_codes, scale_rows = quantize_rows(hidden, received, nblocks)
    owners = lax.axis_size("dp")
    owned_rows = local_hidden // owners
    codes_in, scales_in = (
        lax.all_to_all(
            grad_codes.reshape(owners, owned_rows, full_width),
            "dp",
            split_axis=0,
            concat_axis=0,
            tiled=True,
        ),
        lax.all_to_all(
            scale_rows.reshape(owners, owned_rows, nblocks).astype(jnp.bfloat16),
            "dp",
            split_axis=0,
            concat_axis=0,
            tiled=True,
        ).astype(jnp.float32),
    )
    terms = (
        codes_in.astype(jnp.float32).reshape(owners, owned_rows, nblocks, full_width // nblocks)
        * scales_in[:, :, :, None]
    )
    total_tokens = group_rows * owners
    weight_grad = jnp.sum(terms, axis=0).reshape(owned_rows, full_width) * float(total_tokens) ** (
        -0.5
    )
    return (layer_out, gate_grad, up_grad, weight_grad)


def solution(mesh):
    return jax.shard_map(
        body,
        mesh=mesh,
        in_specs=(
            P("dp", "tensor"),
            P("dp", "tensor"),
            P(("tensor", "dp"), None),
            P(("tensor", "dp"), None),
            P(("dp", "tensor"), None),
        ),
        out_specs=(
            P(("dp", "tensor"), None),
            P("dp", "tensor"),
            P("dp", "tensor"),
            P(("tensor", "dp"), None),
        ),
        check_vma=False,
    )
```

profile of v0, /device:TPU:0, one launch (start us, length us, event | category | flops | bytes accessed | tf_op | source)
XLA Modules:
  0.0 784.0 jit_solution(16857989771824696770)
XLA Ops:
  7.2 0.7 all-gather.6.cloned.1.call-update
  8.0 0.7 all-gather.4.cloned.1.call-update
  8.7 0.8 convert_bitcast_fusion
  9.5 32.3 %all-gather = bf16[8,400,10]{1,2,0:T(8,128)(2,1)S(1)} all-gather(bf16[1,400,10]{1,2,0:T(8,128)(2,1)S(1)} %convert_bitcast_fusion), channel_id=1, replica_groups=mesh['dp'=8,'tensor'=4] {'dp'}, dimensions={0}, use_global_device_ids=true | all-gather | bytes 72000 | tf_op jit(solution)/shard_map/all_gather | solution.py:51
  41.7 0.7 copy_convert_fusion
  42.5 1.1 reshape.47
  43.6 2.2 copy.49
  45.8 2.2 copy.50
  48.0 1.6 copy.53
  49.6 205.9 %all-gather.4.cloned.1.call-done = bf16[3200,2560]{1,0:T(8,128)(2,1)} async-done(((bf16[400,2560]{1,0:T(8,128)(2,1)}), bf16[3200,2560]{1,0:T(8,128)(2,1)}) %all-gather.4.cloned.1.call-update) | async-done | bytes 16384016 | tf_op jit(solution)/shard_map/all_gather | solution.py:50
  255.5 21.9 %copy.51 = bf16[3200,2560]{0,1:T(8,128)(2,1)} copy(bf16[3200,2560]{1,0:T(8,128)(2,1)} %all-gather.4.cloned.1.call-done) | data formatting | bytes 32768000 | tf_op jit(solution)/shard_map/all_gather | solution.py:50
  277.4 9.6 %fusion.4 = bf16[3200,2560]{0,1:T(8,128)(2,1)S(1)} fusion(bf16[3200,2560]{0,1:T(8,128)(2,1)} %copy.51, f32[3200,10]{0,1:T(8,128)S(1)} %reshape.47), kind=kLoop, calls=%fused_computation.10 | loop fusion | flops 24576000 | bytes 32896000 | tf_op jit(solution)/shard_map/convert_element_type | solution.py:19
  287.0 11.8 %multiply_convert_fusion = (bf16[256,3200]{0,1:T(8,128)(2,1)}, bf16[256,3200]{0,1:T(8,128)(2,1)}, bf16[256,3200]{0,1:T(8,128)(2,1)S(1)}) fusion(bf16[256,3200]{0,1:T(8,128)(2,1)} %copy.49, bf16[256,3200]{0,1:T(8,128)(2,1)} %copy.50, bf16[3200,2560]{0,1:T(8,128)(2,1)S(1)} %fusion.4, bf16[256,2560]{1,0:T(8,128)(2,1)} %all-gather.6.cloned.1.call-done), kind=kOutput, calls=%fused_computation.27 | convolution fusion | flops 4208230400 | bytes 25886720 | tf_op jit(solution)/shard_map/dot_general | solution.py:62
  298.8 91.2 %while.12 = (s32[]{:T(128)}, bf16[4,800,2560]{2,1,0:T(8,128)(2,1)}, bf16[4,800,10]{1,2,0:T(8,128)(2,1)S(1)}, bf16[4,256,800]{1,2,0:T(8,128)(2,1)S(1)}, bf16[256,2560]{0,1:T(8,128)(2,1)S(1)}, /*index=5*/s32[]{:T(128)}) while((s32[]{:T(128)}, bf16[4,800,2560]{2,1,0:T(8,128)(2,1)}, bf16[4,800,10]{1,2,0:T(8,128)(2,1)S(1)}, ...), condition=%wide.region_3.4_spmd, body=%wide.region_1.3_spmd.sunk | while | flops 1056792000 | bytes 47019096 | solution.py:37
  298.8 1.7 abs_reduce_fusion.2
  300.5 2.6 divide_convert_fusion.2
  303.1 7.0 copy.67
  310.1 7.1 copy.68
  317.2 4.4 constant_dynamic-update-slice_fusion.2
  321.6 1.7 abs_reduce_fusion.2
  323.3 2.6 divide_convert_fusion.2
  325.9 7.0 copy.67
  332.9 7.1 copy.68
  340.0 4.5 constant_dynamic-update-slice_fusion.2
  344.4 1.7 abs_reduce_fusion.2
  346.1 2.6 divide_convert_fusion.2
  348.8 7.0 copy.67
  355.7 7.1 copy.68
  362.8 4.4 constant_dynamic-update-slice_fusion.2
  367.2 1.7 abs_reduce_fusion.2
  368.9 2.6 divide_convert_fusion.2
  371.5 7.0 copy.67
  378.5 7.1 copy.68
  385.6 4.4 constant_dynamic-update-slice_fusion.2
  390.2 0.2 reshape.49
  390.3 9.5 %all_to_all.10 = bf16[8,2,2000]{2,1,0:T(2,128)(2,1)S(1)} all-to-all(bf16[8,2,2000]{2,1,0:T(2,128)(2,1)S(1)} %reshape.49), channel_id=1, replica_groups=mesh['dp'=8,'tensor'=4] {'dp'}, dimensions={0} | all-to-all | bytes 128000 | tf_op jit(solution)/shard_map/all_to_all | solution.py:80
  399.8 5.7 all-to-all-start
  405.6 0.2 all-reduce.2.cloned.1.call-start
  405.8 9.8 %convolution_convert_fusion = bf16[256,2560]{1,0:T(8,128)(2,1)} fusion(bf16[256,3200]{0,1:T(8,128)(2,1)S(1)} %bitcast.53, bf16[3200,2560]{0,1:T(8,128)(2,1)} %copy-done), kind=kOutput, calls=%fused_computation.18 | convolution fusion | flops 4194959360 | bytes 19333120 | tf_op jit(solution)/shard_map/dot_general | solution.py:56
  415.7 3.8 copy.59
  419.5 2.3 copy.58
  421.8 0.2 reshape.50
  422.0 13.9 %mul.63 = f32[8,400,10,256]{1,3,2,0:T(8,128)} broadcast(bf16[8,400,10]{1,2,0:T(8,128)(2,1)S(1)} %bitcast.54), dimensions={0,1,2} | broadcast | bytes 32832000 | tf_op jit(solution)/shard_map/mul | solution.py:89
  435.9 38.1 %copy.57 = f32[8,400,2560]{2,1,0:T(8,128)} copy(f32[8,400,2560]{1,2,0:T(8,128)} %bitcast.49) | data formatting | bytes 65536000 | tf_op jit(solution)/shard_map/mul | solution.py:89
  474.0 1.7 convert_convert_fusion
  475.7 283.2 %all-to-all-done = bf16[8,400,2560]{2,1,0:T(8,128)(2,1)} async-done(((bf16[8,400,2560]{2,1,0:T(8,128)(2,1)}), bf16[8,400,2560]{2,1,0:T(8,128)(2,1)}, u32[]{:S(2)}, u32[]{:S(2)}) %all-to-all-start) | async-done | bytes 16384032 | tf_op jit(solution)/shard_map/all_to_all | solution.py:73
  758.9 16.2 %multiply_reduce_fusion = f32[400,2560]{1,0:T(8,128)S(1)} fusion(f32[8,400,2560]{2,1,0:T(8,128)} %copy.57, bf16[8,400,2560]{2,1,0:T(8,128)(2,1)} %all-to-all-done), kind=kLoop, calls=%fused_computation.11 | loop fusion | flops 23552000 | bytes 53248000 | tf_op jit(solution)/shard_map/reduce_sum | solution.py:93
  775.2 2.3 broadcast_multiply_fusion
  (28 shorter events, 0.4 us)
Async XLA Ops:
  7.2 36.4 %copy-start.1 = (bf16[256,3200]{1,0:T(8,128)(2,1)S(1)}, bf16[256,3200]{1,0:T(8,128)(2,1)}, u32[]{:S(2)}) copy-start(bf16[256,3200]{1,0:T(8,128)(2,1)} %param.7) | copy-start | bytes 4915204
  7.2 38.6 %copy-start.2 = (bf16[256,3200]{1,0:T(8,128)(2,1)S(1)}, bf16[256,3200]{1,0:T(8,128)(2,1)}, u32[]{:S(2)}) copy-start(bf16[256,3200]{1,0:T(8,128)(2,1)} %param.8) | copy-start | bytes 4915204
  7.2 40.8 %all-gather.6.cloned.1.call-start = ((), (), s32[]{:S(2)}) async-start(), calls=%async_computation.4 | async-start | bytes 1638400 | tf_op jit(solution)/shard_map/all_gather | solution.py:61
  7.9 247.6 %all-gather.4.cloned.1.call-start = ((), (), s32[]{:S(2)}) async-start(), calls=%async_computation.2 | async-start | bytes 18432000 | tf_op jit(solution)/shard_map/all_gather | solution.py:50
  287.0 11.8 %copy-start = (bf16[3200,2560]{0,1:T(8,128)(2,1)}, bf16[3200,2560]{0,1:T(8,128)(2,1)S(1)}, u32[]{:S(2)}) copy-start(bf16[3200,2560]{0,1:T(8,128)(2,1)S(1)} %fusion.4) | copy-start | bytes 49152004
  287.0 11.8 %copy-start.4 = (bf16[4,800,10]{1,2,0:T(8,128)(2,1)S(1)}, bf16[4,800,10]{1,2,0:T(8,128)(2,1)}, u32[]{:S(2)}) copy-start(bf16[4,800,10]{1,2,0:T(8,128)(2,1)} %custom-call.1) | copy-start | bytes 192004
  399.8 359.1 %all-to-all-start = ((bf16[8,400,2560]{2,1,0:T(8,128)(2,1)}), bf16[8,400,2560]{2,1,0:T(8,128)(2,1)}, u32[]{:S(2)}, u32[]{:S(2)}) async-start(bf16[8,400,2560]{2,1,0:T(8,128)(2,1)} %bitcast.51), calls=%async_computation | async-start | bytes 32768000 | tf_op jit(solution)/shard_map/all_to_all | solution.py:73
  405.6 68.5 %all-reduce.2.cloned.1.call-start = ((), (), s32[]{:S(2)}) async-start(), calls=%async_computation.3 | async-start | bytes 2621440 | tf_op jit(solution)/shard_map/psum | solution.py:57
  415.6 3.8 copy-start.3
Sparse Core Ops, SparseCore 0:
  9.6 20.8 all-gather.5
  32.7 222.7 all-gather.3
  415.8 39.9 all-reduce.1
where the time goes:
time: 787 us; the launch traced here: 784 us
  waiting for transfers between devices  490 us (62%)
  local copies, waits for them, and re-layouts  162 us (21%)
  other arithmetic  41.9 us (5%)
  blocking collectives  41.8 us (5%)
  matrix products  28.3 us (4%)
  between operations  13.9 us (2%)
    all_to_all x1, waiting for transfers between devices, body(): lax.all_to_all(grad_codes.reshape(owners, owned_rows, full_width), 'dp',...  283 us
    all_gather x1, waiting for transfers between devices, body(): lax.all_gather(down_codes, 'dp', axis=0, tiled=True)  206 us
    mul x2, local copies, waits for them, and re-layouts, body(): codes_in.astype(jnp.float32)  52.1 us
    dynamic_update_slice x8, local copies, waits for them, and re-layouts, quantize_rows(): grad_codes, scale_rows = lax.map(one_block, stacked)  46 us
    all_gather x1, blocking collectives, body(): lax.all_gather(down_scales.astype(jnp.bfloat16), 'dp', axis=0, tiled=True)  32.3 us
    convert_element_type x4, local copies, waits for them, and re-layouts, one_block(): grad_codes = (blocks / scale_rows[:, :, None]).astype(jnp.bfloat16)  27.9 us
    all_gather x1, local copies, waits for them, and re-layouts, body(): lax.all_gather(down_codes, 'dp', axis=0, tiled=True)  21.9 us
    reduce_sum x1, other arithmetic, body(): jnp.sum(terms, axis=0).reshape(owned_rows, full_width)  16.2 us
  transfers between devices with their start and end apart: 4, of which 2 were waited for; matrix products, arithmetic and copies ran while one was open for 10% of the time, Pallas kernels for 0%

commit v1 on v0

v1 whole, which is shorter than its diff:
```python
import jax
import jax.numpy as jnp
from jax import lax
from jax.sharding import Mesh, PartitionSpec as P


def dequantize(codes, scales):
    rows, width = codes.shape
    nblocks = scales.shape[1]
    blocks = codes.astype(jnp.float32).reshape(rows, nblocks, width // nblocks) * scales[:, :, None]
    return blocks.reshape(rows, width).astype(jnp.bfloat16)


def swap(value, axis):
    return lax.ppermute(value, axis, [(0, 1), (1, 0)])


def gather_pair(value, axis):
    if lax.axis_size(axis) != 2:
        return lax.all_gather(value, axis, axis=0)
    other = swap(value, axis)
    first = lax.axis_index(axis) == 0
    return jnp.stack([jnp.where(first, value, other), jnp.where(first, other, value)])


def scatter_sum(parts, axis):
    size = lax.axis_size(axis)
    if size == 1:
        return parts[0].astype(jnp.float32)
    if size != 2:
        received = lax.all_to_all(parts.astype(jnp.bfloat16), axis, 0, 0, tiled=True)
        return jnp.sum(received.astype(jnp.float32), axis=0)
    me = lax.axis_index(axis)
    theirs = lax.dynamic_index_in_dim(parts, 1 - me, 0, keepdims=False).astype(jnp.bfloat16)
    mine = lax.dynamic_index_in_dim(parts, me, 0, keepdims=False)
    return mine.astype(jnp.float32) + swap(theirs, axis).astype(jnp.float32)


def body(gate_pre, up_pre, down_codes, down_scales, cotangent):
    group_rows, local_hidden = gate_pre.shape
    owned, width = down_codes.shape
    nz, nx, ny, nc = (lax.axis_size(name) for name in ("z", "x", "y", "c"))
    rows = cotangent.shape[0]
    units = nx * owned
    total_tokens = group_rows * nz * nx

    gate_value = gate_pre.astype(jnp.float32)
    up_value = up_pre.astype(jnp.float32)
    sigmoid_gate = jax.nn.sigmoid(gate_value)
    activated = gate_value * sigmoid_gate
    hidden = (activated * up_value).astype(jnp.bfloat16)

    sent = hidden.T.reshape(nz, units, group_rows)
    columns = lax.all_to_all(sent, "z", 0, 0, tiled=True) if nz > 1 else sent

    line = lax.all_gather(cotangent, ("z", "y"), axis=0)
    both = gather_pair(line, "c")
    received = jnp.moveaxis(both, 0, 1).reshape(nz, group_rows, width)

    weight = gather_pair(dequantize(down_codes, down_scales), "x").reshape(units, width)

    partial_out = lax.dot_general(
        columns, weight, (((1,), (0,)), ((), ())), preferred_element_type=jnp.float32
    ).astype(jnp.bfloat16)
    partial_out = partial_out.reshape(nz, ny, nc, rows, width)
    over_c = scatter_sum(jnp.moveaxis(partial_out, 2, 0), "c")
    over_y = scatter_sum(jnp.moveaxis(over_c.astype(jnp.bfloat16), 1, 0), "y")
    layer_out = scatter_sum(over_y.astype(jnp.bfloat16), "z").astype(jnp.bfloat16)

    dcolumns = lax.dot_general(
        weight, received, (((1,), (2,)), ((), ())), preferred_element_type=jnp.float32
    ).astype(jnp.bfloat16)
    dcolumns = jnp.moveaxis(dcolumns, 1, 0)
    back = lax.all_to_all(dcolumns, "z", 0, 0, tiled=True) if nz > 1 else dcolumns
    dhidden = back.reshape(local_hidden, group_rows).T.astype(jnp.float32)
    gate_grad = (
        dhidden * up_value * sigmoid_gate * (1.0 + gate_value * (1.0 - sigmoid_gate))
    ).astype(jnp.bfloat16)
    up_grad = (dhidden * activated).astype(jnp.bfloat16)

    partial_grad = lax.dot_general(
        columns, received, (((0, 2), (0, 1)), ((), ())), preferred_element_type=jnp.float32
    )
    weight_grad = scatter_sum(partial_grad.reshape(nx, owned, width), "x") * float(total_tokens) ** (-0.5)
    return layer_out, gate_grad, up_grad, weight_grad


def outer_split(mesh, tokens, hidden, width):
    dp, tensor = mesh.shape["dp"], mesh.shape["tensor"]

    def rows_sent(nz):
        moved = 2 * (tokens // dp) * (hidden // tensor) / width if nz > 1 else 0
        return 2 * hidden // (tensor * nz) + 2 * tokens * nz // dp + moved

    return min((nz for nz in range(1, dp + 1) if dp % nz == 0), key=rows_sent)


def solution(mesh):
    def call(gate_pre, up_pre, down_codes, down_scales, cotangent):
        tokens, hidden = gate_pre.shape
        nz = outer_split(mesh, tokens, hidden, cotangent.shape[1])
        dp, tensor = mesh.shape["dp"], mesh.shape["tensor"]
        fine = Mesh(mesh.devices.reshape(nz, dp // nz, tensor // 2, 2), ("z", "x", "y", "c"))
        act = P(("z", "x"), ("y", "c"))
        weight = P(("y", "c", "z", "x"), None)
        layer = P(("z", "x", "y", "c"), None)
        return jax.shard_map(
            body,
            mesh=fine,
            in_specs=(act, act, weight, weight, layer),
            out_specs=(layer, act, act, weight),
            check_vma=False,
        )(gate_pre, up_pre, down_codes, down_scales, cotangent)

    return call
```

time: 787 us -> 290 us (0.37)
  waiting for transfers between devices: 490 us -> 135 us
  local copies, waits for them, and re-layouts: 162 us -> 37.5 us
  other arithmetic: 41.9 us -> 29.1 us
  matrix products: 28.3 us -> 19.4 us
    all_to_all x1 -> x2, waiting for transfers between devices: 283 us -> 42.1 us  [the longest x1 37.7 us: body(): columns = lax.all_to_all(sent, 'z', 0, 0, tiled=True) if nz > 1 else sent]
    all_gather x2 -> x1, waiting for transfers between devices: 206 us -> 47.8 us  [body(): line = lax.all_gather(cotangent, ('z', 'y'), axis=0)]
    mul x2 -> x0, local copies, waits for them, and re-layouts: 52.1 us -> none  [body(): codes_in.astype(jnp.float32)]
    dynamic_update_slice x8 -> x0, local copies, waits for them, and re-layouts: 46 us -> none  [quantize_rows(): grad_codes, scale_rows = lax.map(one_block, stacked)]
    ppermute x0 -> x5, waiting for transfers between devices: none -> 44.2 us  [swap(): return lax.ppermute(value, axis, [(0, 1), (1, 0)])]
    all_to_all x1, blocking collectives: 9.49 us -> 42 us  [body(): lax.all_to_all(dcolumns, 'z', 0, 0, tiled=True)]
    all_gather x1 -> x0, blocking collectives: 32.3 us -> none  [body(): lax.all_gather(down_scales.astype(jnp.bfloat16), 'dp', axis=0, tiled=True)]
    all_gather x1 -> x0, local copies, waits for them, and re-layouts: 21.9 us -> none  [body(): lax.all_gather(down_codes, 'dp', axis=0, tiled=True)]
  transfers between devices with their start and end apart: 4 -> 8, of which waited for: 2 -> 6; matrix products, arithmetic and copies ran while one was open for 10% -> 14% of each run, Pallas kernels for 0% -> 0%
where the time goes in v1:
time: 290 us; the launch traced here: 289 us
  waiting for transfers between devices  135 us (47%)
  blocking collectives  42 us (14%)
  local copies, waits for them, and re-layouts  37.5 us (13%)
  other arithmetic  29.1 us (10%)
  matrix products  19.4 us (7%)
  between operations  14.2 us (5%)
  starting transfers between devices  12.2 us (4%)
    all_gather x1, waiting for transfers between devices, body(): line = lax.all_gather(cotangent, ('z', 'y'), axis=0)  47.8 us
    ppermute x5, waiting for transfers between devices, swap(): return lax.ppermute(value, axis, [(0, 1), (1, 0)])  44.2 us
    all_to_all x1, blocking collectives, body(): lax.all_to_all(dcolumns, 'z', 0, 0, tiled=True)  42 us
    all_to_all x1, waiting for transfers between devices, body(): columns = lax.all_to_all(sent, 'z', 0, 0, tiled=True) if nz > 1 else sent  37.7 us
    unnamed x17, local copies, waits for them, and re-layouts  13.2 us
    dot_general x1, matrix products, body(): lax.dot_general(columns, weight, (((1,), (0,)), ((), ())), preferred_elem...  8.62 us
    another operation x4, other arithmetic, gather_pair(): jnp.stack([jnp.where(first, value, other), jnp.where(first, other, value)])  7.67 us
    another operation x1, local copies, waits for them, and re-layouts, gather_pair(): jnp.stack([jnp.where(first, value, other), jnp.where(first, other, value)])  7.55 us
  transfers between devices with their start and end apart: 8, of which 6 were waited for; matrix products, arithmetic and copies ran while one was open for 14% of the time, Pallas kernels for 0%

profile of v1, /device:TPU:0, one launch (start us, length us, event | category | flops | bytes accessed | tf_op | source)
XLA Modules:
  0.0 289.2 jit_solution(6860275836043006170)
XLA Ops:
  7.2 0.0 all-gather.3.cloned.1.call-start
  7.2 0.7 all-gather.3.cloned.1.call-update
  7.9 4.3 %copy.21 = bf16[400,2560]{0,1:T(8,128)(2,1)} copy(bf16[400,2560]{1,0:T(8,128)(2,1)} %param.7) | data formatting | bytes 4096000 | tf_op args[2]
  12.2 2.3 fusion.1
  14.4 2.5 copy.22
  16.9 2.9 %collective-permute-start = (bf16[400,2560]{1,0:T(8,128)(2,1)}, bf16[400,2560]{1,0:T(8,128)(2,1)}, u32[]{:S(2)}, u32[]{:S(2)}) collective-permute-start(bf16[400,2560]{1,0:T(8,128)(2,1)} %copy.22), channel_id=1, source_target_pairs={{0,4},{4,0},{1,5},{5,1},{2,6},{6,2},{3,7},{7,3},{8,12},{12,8},{9,1... | collective-permute-start | bytes 6144008 | tf_op jit(solution)/shard_map/ppermute | solution.py:15
  19.8 47.8 %all-gather.3.cloned.1.call-done = bf16[512,2560]{1,0:T(8,128)(2,1)} async-done(((bf16[64,2560]{1,0:T(8,128)(2,1)}), bf16[512,2560]{1,0:T(8,128)(2,1)}) %all-gather.3.cloned.1.call-update) | async-done | bytes 2621456 | tf_op jit(solution)/shard_map/all_gather | solution.py:56
  67.6 0.0 collective-permute-start.3
  67.6 0.0 collective-permute-done
  67.6 4.3 %copy.23 = bf16[400,2560]{0,1:T(8,128)(2,1)} copy(bf16[400,2560]{1,0:T(8,128)(2,1)} %collective-permute-done) | data formatting | bytes 4096000 | tf_op jit(solution)/shard_map/ppermute | solution.py:15
  71.9 2.1 select_bitcast_fusion.3
  73.9 3.0 %pad_maximum_fusion = bf16[2,400,2560]{1,2,0:T(8,128)(2,1)} fusion(bf16[1,400,2560]{1,2,0:T(8,128)(2,1)S(1)} %get-tuple-element.7, bf16[1,400,2560]{1,2,0:T(8,128)(2,1)S(1)} %get-tuple-element.6), kind=kLoop, calls=%fused_computation.2 | loop fusion | flops 2048000 | bytes 8192000 | tf_op jit(solution)/shard_map/stack | solution.py:23
  77.0 7.6 %copy.25 = bf16[2,400,2560]{2,1,0:T(8,128)(2,1)} copy(bf16[2,400,2560]{1,2,0:T(8,128)(2,1)} %pad_maximum_fusion) | data formatting | bytes 8192000 | tf_op jit(solution)/shard_map/stack | solution.py:23
  84.5 0.0 collective-permute-done.3
  84.5 2.1 select_bitcast_fusion.1
  86.6 0.0 copy-start.3
  86.6 0.5 pad_maximum_fusion.1
  87.1 3.4 %copy-done.3 = bf16[2,400,2560]{2,1,0:T(8,128)(2,1)S(1)} copy-done((bf16[2,400,2560]{2,1,0:T(8,128)(2,1)S(1)}, bf16[2,400,2560]{2,1,0:T(8,128)(2,1)}, u32[]{:S(2)}) %copy-start.3) | copy-done | bytes 4096024
  90.6 4.4 %fusion.15 = bf16[4,800,256]{2,1,0:T(8,128)(2,1)S(1)} fusion(bf16[800,2560,1]{1,0,2:T(8,128)(2,1)S(1)} %bitcast.71, bf16[4,256,2560]{2,1,0:T(8,128)(2,1)S(1)} %bitcast.66), kind=kOutput, calls=%fused_computation.37 | convolution fusion | flops 4195123200 | bytes 10977280 | tf_op jit(solution)/shard_map/dot_general | solution.py:70
  95.0 42.0 %all_to_all.15 = bf16[4,800,256]{2,1,0:T(8,128)(2,1)S(1)} all-to-all(bf16[4,800,256]{2,1,0:T(8,128)(2,1)S(1)} %fusion.15), channel_id=1, replica_groups=mesh['z'=4,'x'=2,'y'=2,'c'=2] {'z'}, dimensions={0} | all-to-all | bytes 3276800 | tf_op jit(solution)/shard_map/all_to_all | solution.py:74
  137.0 2.1 bitcast_convert_fusion
  139.1 3.4 %copy.27 = f32[3200,256]{0,1:T(8,128)S(1)} copy(f32[3200,256]{1,0:T(8,128)} %bitcast_convert_fusion) | data formatting | bytes 6553600 | tf_op jit(solution)/shard_map/convert_element_type | solution.py:75
  142.5 4.7 %fusion.11 = (bf16[256,3200]{1,0:T(8,128)(2,1)}, bf16[256,3200]{1,0:T(8,128)(2,1)}, bf16[3200,256]{0,1:T(8,128)(2,1)}) fusion(f32[3200,256]{0,1:T(8,128)S(1)} %copy.27, bf16[256,3200]{1,0:T(8,128)(2,1)} %param.5, bf16[256,3200]{1,0:T(8,128)(2,1)} %param.6), kind=kLoop, calls=%fused_computation.25 | loop fusion | flops 13926400 | bytes 11468800 | tf_op jit(solution)/shard_map/convert_element_type | solution.py:79
  147.2 3.7 %copy.20 = bf16[3200,256]{1,0:T(8,128)(2,1)} copy(bf16[3200,256]{0,1:T(8,128)(2,1)} %get-tuple-element.10) | data formatting | bytes 3276800 | tf_op jit(solution)/shard_map/transpose | solution.py:53
  150.9 3.7 %all-to-all-start = ((bf16[4,800,256]{2,1,0:T(8,128)(2,1)}), bf16[4,800,256]{2,1,0:T(8,128)(2,1)S(1)}, u32[]{:S(2)}, u32[]{:S(2)}) async-start(bf16[4,800,256]{2,1,0:T(8,128)(2,1)} %bitcast.1), calls=%async_computation | async-start | bytes 3276800 | tf_op jit(solution)/shard_map/all_to_all | solution.py:54
  154.7 37.7 %all-to-all-done = bf16[4,800,256]{2,1,0:T(8,128)(2,1)S(1)} async-done(((bf16[4,800,256]{2,1,0:T(8,128)(2,1)}), bf16[4,800,256]{2,1,0:T(8,128)(2,1)S(1)}, u32[]{:S(2)}, u32[]{:S(2)}) %all-to-all-start) | async-done | bytes 1638432 | tf_op jit(solution)/shard_map/all_to_all | solution.py:54
  192.4 8.6 %convolution_convert_fusion = bf16[4,256,2560]{2,1,0:T(8,128)(2,1)S(1)} fusion(bf16[4,800,256]{2,1,0:T(8,128)(2,1)S(1)} %all-to-all-done, bf16[800,2560,1]{1,0,2:T(8,128)(2,1)} %bitcast.70), kind=kOutput, calls=%fused_computation.1 | convolution fusion | flops 4196925440 | bytes 10977280 | tf_op jit(solution)/shard_map/dot_general | solution.py:62
  201.0 0.2 dynamic-slice_bitcast_fusion
  201.2 2.2 copy-done.1
  203.4 0.0 collective-permute-start.1
  203.4 5.0 %collective-permute-done.1 = bf16[4,2,64,2560]{3,2,1,0:T(8,128)(2,1)} collective-permute-done((bf16[4,2,64,2560]{3,2,1,0:T(8,128)(2,1)S(1)}, bf16[4,2,64,2560]{3,2,1,0:T(8,128)(2,1)}, u32[]{:S(2)}, u32[]{:S(2)}) %collective-permute-start.1) | collective-permute-done | bytes 2621472 | tf_op jit(solution)/shard_map/ppermute | solution.py:15
  208.4 3.2 %fusion = bf16[4,2,64,2560]{3,2,1,0:T(8,128)(2,1)S(1)} fusion(bf16[4,2,64,2560]{3,2,1,0:T(8,128)(2,1)} %collective-permute-done.1, bf16[4,2,2,64,2560]{4,3,2,1,0:T(8,128)(2,1)} %bitcast.69, s32[]{:T(128)S(6)} %select_n.48), kind=kLoop, calls=%fused_computation.5 | loop fusion | flops 5242880 | bytes 7864324 | tf_op jit(solution)/shard_map/convert_element_type | solution.py:67
  211.6 0.0 copy-start.6
  211.7 1.2 dynamic-slice_bitcast_fusion.1
  212.9 0.5 collective-permute-start.2
  213.4 0.2 copy-done.6
  213.5 6.3 %convolution_bitcast_fusion = f32[2,400,2560]{2,1,0:T(8,128)S(1)} fusion(bf16[2,400,4,256]{3,1,0,2:T(8,128)(2,1)S(1)} %bitcast.74, bf16[4,256,2560,1]{2,1,3,0:T(8,128)(2,1)} %bitcast.67), kind=kOutput, calls=%fused_computation | convolution fusion | flops 4194304000 | bytes 15073280 | tf_op jit(solution)/shard_map/dot_general | solution.py:81
  219.9 0.0 copy-start.2
  219.9 3.2 %copy-done.2 = f32[2,400,2560]{2,1,0:T(8,128)} copy-done((f32[2,400,2560]{2,1,0:T(8,128)}, f32[2,400,2560]{2,1,0:T(8,128)S(1)}, u32[]{:S(2)}) %copy-start.2) | copy-done | bytes 8192024
  223.1 1.5 fusion.13
  224.6 1.5 collective-permute-start.4
  226.0 18.0 %collective-permute-done.2 = bf16[4,64,2560]{2,1,0:T(8,128)(2,1)} collective-permute-done((bf16[4,64,2560]{2,1,0:T(8,128)(2,1)}, bf16[4,64,2560]{2,1,0:T(8,128)(2,1)}, u32[]{:S(2)}, u32[]{:S(2)}) %collective-permute-start.2) | collective-permute-done | bytes 1310752 | tf_op jit(solution)/shard_map/ppermute | solution.py:15
  244.0 2.7 fusion.12
  246.7 3.5 %all-to-all-start.1 = ((bf16[4,64,2560]{2,1,0:T(8,128)(2,1)}), bf16[4,64,2560]{2,1,0:T(8,128)(2,1)S(1)}, u32[]{:S(2)}, u32[]{:S(2)}) async-start(bf16[4,64,2560]{2,1,0:T(8,128)(2,1)} %fusion.12), calls=%async_computation.1 | async-start | bytes 2621440 | tf_op jit(solution)/shard_map/all_to_all | solution.py:31
  250.3 21.2 %collective-permute-done.4 = bf16[400,2560]{1,0:T(8,128)(2,1)} collective-permute-done((bf16[400,2560]{1,0:T(8,128)(2,1)}, bf16[400,2560]{1,0:T(8,128)(2,1)}, u32[]{:S(2)}, u32[]{:S(2)}) %collective-permute-start.4) | collective-permute-done | bytes 2048032 | tf_op jit(solution)/shard_map/ppermute | solution.py:15
  271.5 5.4 %fusion.2 = f32[400,2560]{1,0:T(8,128)} fusion(bf16[400,2560]{1,0:T(8,128)(2,1)} %collective-permute-done.4, f32[2,400,2560]{2,1,0:T(8,128)} %copy-done.2, s32[]{:T(128)S(6)} %select_n.55), kind=kLoop, calls=%fused_computation.12 | loop fusion | flops 3072000 | bytes 10240004 | tf_op jit(solution)/shard_map/mul | solution.py:84
  276.9 4.4 %all-to-all-done.1 = bf16[4,64,2560]{2,1,0:T(8,128)(2,1)S(1)} async-done(((bf16[4,64,2560]{2,1,0:T(8,128)(2,1)}), bf16[4,64,2560]{2,1,0:T(8,128)(2,1)S(1)}, u32[]{:S(2)}, u32[]{:S(2)}) %all-to-all-start.1) | async-done | bytes 1310752 | tf_op jit(solution)/shard_map/all_to_all | solution.py:31
  281.3 1.0 reduce_sum.12
  (9 shorter events, 0.0 us)
Async XLA Ops:
  7.2 5.0 %copy-start.7 = (f32[400,10]{0,1:T(8,128)S(1)}, f32[400,10]{0,1:T(8,128)}, u32[]{:S(2)}) copy-start(f32[400,10]{0,1:T(8,128)} %param.8) | copy-start | bytes 48004
  7.2 60.4 %all-gather.3.cloned.1.call-start = ((), (), s32[]{:S(2)}) async-start(), calls=%async_computation.3 | async-start | bytes 2949120 | tf_op jit(solution)/shard_map/all_gather | solution.py:56
  16.9 50.7 %collective-permute-start = (bf16[400,2560]{1,0:T(8,128)(2,1)}, bf16[400,2560]{1,0:T(8,128)(2,1)}, u32[]{:S(2)}, u32[]{:S(2)}) collective-permute-start(bf16[400,2560]{1,0:T(8,128)(2,1)} %copy.22), channel_id=1, source_target_pairs={{0,4},{4,0},{1,5},{5,1},{2,6},{6,2},{3,7},{7,3},{8,12},{12,8},{9,1... | collective-permute-start | bytes 6144008 | tf_op jit(solution)/shard_map/ppermute | solution.py:15
  67.6 16.9 %collective-permute-start.3 = (bf16[8,64,2560]{2,1,0:T(8,128)(2,1)}, bf16[8,64,2560]{2,1,0:T(8,128)(2,1)}, u32[]{:S(2)}, u32[]{:S(2)}) collective-permute-start(bf16[8,64,2560]{2,1,0:T(8,128)(2,1)} %bitcast.72), channel_id=1, source_target_pairs={{0,1},{1,0},{2,3},{3,2},{4,5},{5,4},{6,7},{7,6},{8,9},{9,8},{10,11... | collective-permute-start | bytes 7864328 | tf_op jit(solution)/shard_map/ppermute | solution.py:15
  77.0 7.6 %copy-start.4 = (bf16[512,2560]{1,0:T(8,128)(2,1)S(1)}, bf16[512,2560]{1,0:T(8,128)(2,1)}, u32[]{:S(2)}) copy-start(bf16[512,2560]{1,0:T(8,128)(2,1)} %all-gather.3.cloned.1.call-done) | copy-start | bytes 7864324
  86.6 3.9 %copy-start.3 = (bf16[2,400,2560]{2,1,0:T(8,128)(2,1)S(1)}, bf16[2,400,2560]{2,1,0:T(8,128)(2,1)}, u32[]{:S(2)}) copy-start(bf16[2,400,2560]{2,1,0:T(8,128)(2,1)} %copy.25) | copy-start | bytes 12288004
  87.1 7.9 %copy-start = (bf16[2,8,64,2560]{3,2,0,1:T(8,128)(2,1)}, bf16[2,8,64,2560]{3,2,0,1:T(8,128)(2,1)S(1)}, u32[]{:S(2)}) copy-start(bf16[2,8,64,2560]{3,2,0,1:T(8,128)(2,1)S(1)} %pad_maximum_fusion.1) | copy-start | bytes 15728644
  150.9 41.5 %all-to-all-start = ((bf16[4,800,256]{2,1,0:T(8,128)(2,1)}), bf16[4,800,256]{2,1,0:T(8,128)(2,1)S(1)}, u32[]{:S(2)}, u32[]{:S(2)}) async-start(bf16[4,800,256]{2,1,0:T(8,128)(2,1)} %bitcast.1), calls=%async_computation | async-start | bytes 3276800 | tf_op jit(solution)/shard_map/all_to_all | solution.py:54
  192.4 8.6 %copy-start.5 = (bf16[4,800,256]{2,1,0:T(8,128)(2,1)}, bf16[4,800,256]{2,1,0:T(8,128)(2,1)S(1)}, u32[]{:S(2)}) copy-start(bf16[4,800,256]{2,1,0:T(8,128)(2,1)S(1)} %all-to-all-done) | copy-start | bytes 4915204
  201.0 2.4 copy-start.1
  203.4 5.0 %collective-permute-start.1 = (bf16[4,2,64,2560]{3,2,1,0:T(8,128)(2,1)S(1)}, bf16[4,2,64,2560]{3,2,1,0:T(8,128)(2,1)}, u32[]{:S(2)}, u32[]{:S(2)}) collective-permute-start(bf16[4,2,64,2560]{3,2,1,0:T(8,128)(2,1)S(1)} %dynamic-slice_bitcast_fusion), channel_id=1, source_target_pairs={{0,1},{1,0},{2,3},{3,2},{4,5},{5,4},{6,7},{7,6},{8,9},{9,8},{10,11... | collective-permute-start | bytes 7864328 | tf_op jit(solution)/shard_map/ppermute | solution.py:15
  211.6 1.9 copy-start.6
  212.9 31.1 %collective-permute-start.2 = (bf16[4,64,2560]{2,1,0:T(8,128)(2,1)}, bf16[4,64,2560]{2,1,0:T(8,128)(2,1)}, u32[]{:S(2)}, u32[]{:S(2)}) collective-permute-start(bf16[4,64,2560]{2,1,0:T(8,128)(2,1)} %dynamic-slice_bitcast_fusion.1), channel_id=1, source_target_pairs={{0,2},{2,0},{1,3},{3,1},{4,6},{6,4},{5,7},{7,5},{8,10},{10,8},{9,1... | collective-permute-start | bytes 3932168 | tf_op jit(solution)/shard_map/ppermute | solution.py:15
  219.9 3.2 %copy-start.2 = (f32[2,400,2560]{2,1,0:T(8,128)}, f32[2,400,2560]{2,1,0:T(8,128)S(1)}, u32[]{:S(2)}) copy-start(f32[2,400,2560]{2,1,0:T(8,128)S(1)} %convolution_bitcast_fusion) | copy-start | bytes 24576004
  224.6 46.9 %collective-permute-start.4 = (bf16[400,2560]{1,0:T(8,128)(2,1)}, bf16[400,2560]{1,0:T(8,128)(2,1)}, u32[]{:S(2)}, u32[]{:S(2)}) collective-permute-start(bf16[400,2560]{1,0:T(8,128)(2,1)} %fusion.13), channel_id=1, source_target_pairs={{0,4},{4,0},{1,5},{5,1},{2,6},{6,2},{3,7},{7,3},{8,12},{12,8},{9,1... | collective-permute-start | bytes 6144008 | tf_op jit(solution)/shard_map/ppermute | solution.py:15
  246.7 34.6 %all-to-all-start.1 = ((bf16[4,64,2560]{2,1,0:T(8,128)(2,1)}), bf16[4,64,2560]{2,1,0:T(8,128)(2,1)S(1)}, u32[]{:S(2)}, u32[]{:S(2)}) async-start(bf16[4,64,2560]{2,1,0:T(8,128)(2,1)} %fusion.12), calls=%async_computation.1 | async-start | bytes 2621440 | tf_op jit(solution)/shard_map/all_to_all | solution.py:31
Sparse Core Ops, SparseCore 0:
  10.2 57.3 all-gather.2

commit v2 on v1

--- a/solution.py
+++ b/solution.py
@@ -1,7 +1,14 @@
+import functools
+
 import jax
 import jax.numpy as jnp
 from jax import lax
+from jax.experimental import pallas as pl
+from jax.experimental.pallas import tpu as pltpu
 from jax.sharding import Mesh, PartitionSpec as P
+
+VMEM_BYTES = 32 * 2**20
+WEIGHT_COST = 6
 
 
 def dequantize(codes, scales):
@@ -36,6 +43,200 @@
     return mine.astype(jnp.float32) + swap(theirs, axis).astype(jnp.float32)
 
 
+def exchange(value, axis, offset):
+    size = lax.axis_size(axis)
+    return lax.ppermute(value, axis, [(i, i ^ offset) for i in range(size)])
+
+
+def call_kernel(kernel, place, inputs, in_specs, out_shapes, out_specs, grid, scratch, cost):
+    flops, nbytes, transcendentals = cost
+    return pl.pallas_call(
+        kernel,
+        out_shape=out_shapes,
+        grid_spec=pltpu.PrefetchScalarGridSpec(
+            num_scalar_prefetch=1,
+            grid=grid,
+            in_specs=in_specs,
+            out_specs=out_specs,
+            scratch_shapes=scratch,
+        ),
+        compiler_params=pltpu.CompilerParams(vmem_limit_bytes=VMEM_BYTES),
+        cost_estimate=pl.CostEstimate(
+            flops=flops, bytes_accessed=nbytes, transcendentals=transcendentals
+        ),
+    )(place, *inputs)
+
+
+def whole(shape):
+    return pl.BlockSpec(shape, lambda i, place: (0,) * len(shape))
+
+
+def token_start(place, block, rows):
+    return pl.multiple_of(((place[2] ^ (block % 2)) * 2 + (place[3] ^ (block // 2))) * rows, 16)
+
+
+def hidden_kernel(nz, units, place, gate, up, *refs):
+    outs, (natural, columns) = refs[:nz], refs[nz:]
+    step = pl.program_id(0)
+    group, span = gate.shape
+    rows = group // 4
+    value = gate[...].astype(jnp.float32)
+    hidden = value * jax.nn.sigmoid(value) * up[...].astype(jnp.float32)
+    natural[...] = hidden.astype(jnp.bfloat16)
+    ordered = [natural[pl.ds(token_start(place, b, rows), rows), :] for b in range(4)]
+    columns[pl.ds(pl.multiple_of(step * span, 128), span), :] = jnp.concatenate(ordered, axis=0).T
+
+    @pl.when(step == pl.num_programs(0) - 1)
+    def _():
+        half = units // 2
+        for k in range(nz):
+            for r in range(2):
+                start = (place[0] ^ k) * units + (place[1] ^ r) * half
+                outs[k][r * half : (r + 1) * half, :] = columns[
+                    pl.ds(pl.multiple_of(start, 16), half), :
+                ]
+
+
+def weight_kernel(place, codes, scales, other_codes, other_scales, weight):
+    lane = lax.broadcasted_iota(jnp.int32, scales.shape, 1)
+    half = codes.shape[0]
+    for r, (code, scale) in enumerate(((codes, scales), (other_codes, other_scales))):
+        mine = jnp.where(lane == pl.program_id(0), scale[...], 0.0)
+        value = code[...].astype(jnp.float32) * jnp.sum(mine, axis=1, keepdims=True)
+        weight[r * half : (r + 1) * half, :] = value.astype(jnp.bfloat16)
+
+
+def columns_kernel(nz, place, *refs):
+    pieces, (keep, send, mine, theirs) = refs[:nz], refs[nz:]
+    half, group = mine.shape[0], pieces[0].shape[1]
+    rows = group // 4
+    for k in range(nz):
+        turned = pieces[k][...].T
+        for b in range(4):
+            target = send if b >= 2 else keep
+            start = ((b % 2) * nz + k) * rows
+            target[start : start + rows, :] = turned[b * rows : (b + 1) * rows, :]
+        mine[:, k * group : (k + 1) * group] = pieces[k][:half, :]
+        theirs[:, k * group : (k + 1) * group] = pieces[k][half:, :]
+
+
+def grads_kernel(nz, units, place, gate, up, *refs):
+    pieces, (gate_grad, up_grad, columns, natural) = refs[:nz], refs[nz:]
+    step = pl.program_id(0)
+    group, span = gate.shape
+    rows = group // 4
+
+    @pl.when(step == 0)
+    def _():
+        half = units // 2
+        for k in range(nz):
+            for r in range(2):
+                start = (place[0] ^ k) * units + (place[1] ^ r) * half
+                columns[pl.ds(pl.multiple_of(start, 16), half), :] = pieces[k][
+                    r * half : (r + 1) * half, :
+                ]
+
+    ordered = columns[pl.ds(pl.multiple_of(step * span, 128), span), :].T
+    for b in range(4):
+        natural[pl.ds(token_start(place, b, rows), rows), :] = ordered[b * rows : (b + 1) * rows]
+    dhidden = natural[...].astype(jnp.float32)
+    value = gate[...].astype(jnp.float32)
+    up_value = up[...].astype(jnp.float32)
+    sigmoid_gate = jax.nn.sigmoid(value)
+    gate_grad[...] = (
+        dhidden * up_value * sigmoid_gate * (1.0 + value * (1.0 - sigmoid_gate))
+    ).astype(jnp.bfloat16)
+    up_grad[...] = (dhidden * (value * sigmoid_gate)).astype(jnp.bfloat16)
+
+
+def matmul(lhs, rhs, lhs_dim=1, rhs_dim=0, dtype=jnp.float32):
+    dims = (((lhs_dim,), (rhs_dim,)), ((), ()))
+    return lax.dot_general(lhs, rhs, dims, preferred_element_type=jnp.float32).astype(dtype)
+
+
+def paired_body(gate_pre, up_pre, down_codes, down_scales, cotangent):
+    group_rows, local_hidden = gate_pre.shape
+    owned, width = down_codes.shape
+    nz = lax.axis_size("z")
+    rows = cotangent.shape[0]
+    units = 2 * owned
+    total_tokens = group_rows * nz * 2
+    bf16, f32 = jnp.bfloat16, jnp.float32
+    place = jnp.stack([lax.axis_index(name) for name in ("z", "x", "y", "c")]).astype(jnp.int32)
+    struct = jax.ShapeDtypeStruct
+
+    other_codes, other_scales = exchange(down_codes, "x", 1), exchange(down_scales, "x", 1)
+
+    span = column_span(local_hidden)
+    steps = local_hidden // span
+    piece = struct((units, group_rows), bf16)
+    wide = pl.BlockSpec((group_rows, span), lambda i, place: (0, i))
+    act_bytes = group_rows * local_hidden * 2
+    act_scratch = [pltpu.VMEM((group_rows, span), bf16), pltpu.VMEM((local_hidden, group_rows), bf16)]
+    sent = call_kernel(
+        functools.partial(hidden_kernel, nz, units), place, (gate_pre, up_pre), [wide] * 2,
+        [piece] * nz, [whole(piece.shape)] * nz, (steps,), act_scratch,
+        (4 * act_bytes, 3 * act_bytes, act_bytes // 2),
+    )
+
+    line = [exchange(cotangent, "z", k) for k in range(1, nz)]
+    line, sent = lax.optimization_barrier((line, sent))
+    line = jnp.stack([cotangent] + line)
+    columns = [sent[0]] + [exchange(sent[k], "z", k) for k in range(1, nz)]
+    over_y = exchange(line, "y", 1)
+    other_core = exchange(line, "c", 1)
+
+    nblocks = down_scales.shape[1]
+    block = width // nblocks
+    code_block = pl.BlockSpec((owned, block), lambda i, place: (0, i))
+    weight = call_kernel(
+        weight_kernel, place, (down_codes, down_scales, other_codes, other_scales),
+        [code_block, whole(down_scales.shape)] * 2, struct((units, width), bf16),
+        pl.BlockSpec((units, block), lambda i, place: (0, i)), (nblocks,), [],
+        (2 * units * width, WEIGHT_COST * units * width, 0),
+    )
+    over_y, columns, weight = lax.optimization_barrier((over_y, columns, weight))
+    received = (line, over_y, other_core, exchange(over_y, "c", 1))
+    half_tokens = nz * group_rows // 2
+    keep, send, mine, theirs = call_kernel(
+        functools.partial(columns_kernel, nz), place, tuple(columns),
+        [whole(piece.shape)] * nz,
+        [struct((half_tokens, units), bf16)] * 2 + [struct((owned, 2 * half_tokens), bf16)] * 2,
+        [whole((half_tokens, units))] * 2 + [whole((owned, 2 * half_tokens))] * 2, (1,), [],
+        (0, 12 * units * half_tokens, 0),
+    )
+
+    tokens = jnp.stack(received, axis=1).reshape(nz, group_rows, width)
+    back = [matmul(weight, tokens[k], 1, 1, bf16) for k in range(nz)]
+    back = [back[0]] + [exchange(back[k], "z", k) for k in range(1, nz)]
+
+    tokens = tokens.reshape(-1, width)
+    factor = float(total_tokens) ** (-0.5)
+    over_x = exchange((matmul(theirs, tokens) * factor).astype(bf16), "x", 1)
+    weight_grad = matmul(mine, tokens) * factor + over_x.astype(f32)
+
+    over_c = exchange(matmul(send, weight, dtype=bf16), "c", 1)
+    own_c = matmul(keep, weight, dtype=bf16)
+    sums = (own_c.astype(f32) + over_c.astype(f32)).reshape(2, nz, rows, width)
+    over_y = sums[0] + exchange(sums[1].astype(bf16), "y", 1).astype(f32)
+    layer_out = over_y[0]
+    for k in range(1, nz):
+        layer_out = layer_out + exchange(over_y[k].astype(bf16), "z", k).astype(f32)
+    layer_out = layer_out.astype(bf16)
+
+    gate_grad, up_grad = call_kernel(
+        functools.partial(grads_kernel, nz, units), place, (gate_pre, up_pre, *back),
+        [wide] * 2 + [whole(piece.shape)] * nz,
+        [struct((group_rows, local_hidden), bf16)] * 2, [wide] * 2, (steps,), act_scratch[::-1],
+        (12 * act_bytes, 5 * act_bytes, act_bytes // 2),
+    )
+    return layer_out, gate_grad, up_grad, weight_grad
+
+
+def column_span(width):
+    return max((s for s in range(128, 641, 128) if width % s == 0), default=0)
+
+
 def body(gate_pre, up_pre, down_codes, down_scales, cotangent):
     group_rows, local_hidden = gate_pre.shape
     owned, width = down_codes.shape
@@ -104,8 +305,13 @@
         act = P(("z", "x"), ("y", "c"))
         weight = P(("y", "c", "z", "x"), None)
         layer = P(("z", "x", "y", "c"), None)
+        owned = hidden // (dp * tensor)
+        rows = tokens // (dp * tensor)
+        pairs = fine.shape["x"] == 2 and fine.shape["y"] == 2 and nz & (nz - 1) == 0
+        aligned = owned % 16 == 0 and rows % 16 == 0 and column_span(hidden // tensor)
+        block = cotangent.shape[1] // down_scales.shape[1]
         return jax.shard_map(
-            body,
+            paired_body if pairs and aligned and block % 128 == 0 else body,
             mesh=fine,
             in_specs=(act, act, weight, weight, layer),
             out_specs=(layer, act, act, weight),

time: 290 us -> 162 us (0.56)
  waiting for transfers between devices: 135 us -> 70 us
  blocking collectives: 42 us -> 0 us
  local copies, waits for them, and re-layouts: 37.5 us -> 3.88 us
  starting transfers between devices: 12.2 us -> 44.6 us
  other arithmetic: 29.1 us -> 7.84 us
  Pallas kernels: 0 us -> 16.4 us
  between operations: 14.2 us -> 0.87 us
    all_gather x1 -> x0, waiting for transfers between devices: 47.8 us -> none  [body(): line = lax.all_gather(cotangent, ('z', 'y'), axis=0)]
    all_to_all x2 -> x0, waiting for transfers between devices: 42.1 us -> none  [the longest x1 37.7 us: body(): columns = lax.all_to_all(sent, 'z', 0, 0, tiled=True) if nz > 1 else sent]
    all_to_all x1 -> x0, blocking collectives: 42 us -> none  [body(): lax.all_to_all(dcolumns, 'z', 0, 0, tiled=True)]
    ppermute x5 -> x20, starting transfers between devices: 4.91 us -> 44.6 us  [exchange(): return lax.ppermute(value, axis, [(i, i ^ offset) for i in range(size)])]
    ppermute x5 -> x20, waiting for transfers between devices: 44.2 us -> 70 us  [exchange(): return lax.ppermute(value, axis, [(i, i ^ offset) for i in range(size)])]
    pallas_call x0 -> x4, Pallas kernels: none -> 16.4 us  [call_kernel(): pl.pallas_call(kernel, out_shape=out_shapes, grid_spec=pltpu.PrefetchScal...]
    convert_element_type x5 -> x1, other arithmetic: 15 us -> 0.87 us  [paired_body(): layer_out = layer_out.astype(bf16)]
    unnamed x17 -> x19, local copies, waits for them, and re-layouts: 13.2 us -> 3.03 us
  transfers between devices with their start and end apart: 8 -> 20, of which waited for: 6 -> 8; matrix products, arithmetic and copies ran while one was open for 14% -> 16% of each run, Pallas kernels for 0% -> 10%
where the time goes in v2:
time: 162 us; the launch traced here: 161 us
  waiting for transfers between devices  70 us (43%)
  starting transfers between devices  44.6 us (28%)
  matrix products  17.8 us (11%)
  Pallas kernels  16.4 us (10%)
  other arithmetic  7.84 us (5%)
  local copies, waits for them, and re-layouts  3.88 us (2%)
    ppermute x20, waiting for transfers between devices, exchange(): return lax.ppermute(value, axis, [(i, i ^ offset) for i in range(size)])  70 us
    ppermute x20, starting transfers between devices, exchange(): return lax.ppermute(value, axis, [(i, i ^ offset) for i in range(size)])  44.6 us
    dot_general x8, matrix products, matmul(): lax.dot_general(lhs, rhs, dims, preferred_element_type=jnp.float32)  17.8 us
    pallas_call x4, Pallas kernels, call_kernel(): pl.pallas_call(kernel, out_shape=out_shapes, grid_spec=pltpu.PrefetchScal...  16.4 us
    another operation x2, other arithmetic, paired_body(): tokens = jnp.stack(received, axis=1).reshape(nz, group_rows, width)  5.68 us
  transfers between devices with their start and end apart: 20, of which 8 were waited for; matrix products, arithmetic and copies ran while one was open for 16% of the time, Pallas kernels for 10%

profile of v2, /device:TPU:0, one launch (start us, length us, event | category | flops | bytes accessed | tf_op | source)
XLA Modules:
  0.0 161.4 jit_solution(12848545840663799836)
XLA Ops:
  0.6 3.0 %collective-permute-start.7 = (bf16[400,2560]{1,0:T(8,128)(2,1)}, bf16[400,2560]{1,0:T(8,128)(2,1)}, u32[]{:S(2)}, u32[]{:S(2)}) collective-permute-start(bf16[400,2560]{1,0:T(8,128)(2,1)} %codes.1), channel_id=1, source_target_pairs={{0,4},{4,0},{1,5},{5,1},{2,6},{6,2},{3,7},{7,3},{8,12},{12,8},{9,1... | collective-permute-start | bytes 6144008 | tf_op jit(solution)/shard_map/ppermute | solution.py:48
  3.6 1.6 collective-permute-start
  5.2 2.6 %collective-permute-start.1 = (bf16[64,2560]{1,0:T(8,128)(2,1)}, bf16[64,2560]{1,0:T(8,128)(2,1)}, u32[]{:S(2)}, u32[]{:S(2)}) collective-permute-start(bf16[64,2560]{1,0:T(8,128)(2,1)} %param.9), channel_id=1, source_target_pairs={{0,16},{8,24},{16,0},{24,8},{1,17},{9,25},{17,1},{25,9},{2,18},{10... | collective-permute-start | bytes 983048 | tf_op jit(solution)/shard_map/ppermute | solution.py:48
  7.8 0.2 collective-permute-start.2
  8.1 1.4 copy-done
  9.5 1.4 copy-done.2
  11.0 2.8 %shard_map.84 = (bf16[800,256]{1,0:T(8,128)(2,1)S(1)}, bf16[800,256]{1,0:T(8,128)(2,1)S(1)}, bf16[800,256]{1,0:T(8,128)(2,1)S(1)}, bf16[800,256]{1,0:T(8,128)(2,1)S(1)}) custom-call(s32[4]{0:T(128)S(1)} %pad_add_fusion.place, bf16[256,3200]{1,0:T(8,128)(2,1)S(1)} %copy-done, bf16[256,3200]{1,0:T(8,128)(2,1)S(1)} %copy-done.2), custom_call_target="tpu_custom_call" | custom-call | flops 6553600 | bytes 4915200 | tf_op jit(solution)/shard_map/pallas_call | solution.py:53
  13.9 5.4 %collective-permute-done = bf16[64,2560]{1,0:T(8,128)(2,1)} collective-permute-done((bf16[64,2560]{1,0:T(8,128)(2,1)}, bf16[64,2560]{1,0:T(8,128)(2,1)}, u32[]{:S(2)}, u32[]{:S(2)}) %collective-permute-start) | collective-permute-done | bytes 327712 | tf_op jit(solution)/shard_map/ppermute | solution.py:48
  19.2 11.9 %collective-permute-done.1 = bf16[64,2560]{1,0:T(8,128)(2,1)} collective-permute-done((bf16[64,2560]{1,0:T(8,128)(2,1)}, bf16[64,2560]{1,0:T(8,128)(2,1)}, u32[]{:S(2)}, u32[]{:S(2)}) %collective-permute-start.1) | collective-permute-done | bytes 327712 | tf_op jit(solution)/shard_map/ppermute | solution.py:48
  31.1 2.9 %fusion.6 = (bf16[4,1,64,2560]{3,2,1,0:T(8,128)(2,1)}, bf16[4,64,2560]{2,1,0:T(8,128)(2,1)}) fusion(bf16[1,64,2560]{2,1,0:T(8,128)(2,1)} %bitcast.7, bf16[1,64,2560]{2,1,0:T(8,128)(2,1)} %bitcast.6, bf16[1,64,2560]{2,1,0:T(8,128)(2,1)} %bitcast.5, bf16[1,64,2560]{2,1,0:T(8,128)(2,1)S(1)} %bitcast.68), kind=kLoop, calls=%fused_computation.24 | loop fusion | flops 1966080 | bytes 3932160 | tf_op jit(solution)/shard_map/stack | solution.py:209
  34.0 1.5 collective-permute-start.3
  35.5 0.1 copy.12.scales
  35.7 0.6 collective-permute-start.8
  36.3 5.9 %collective-permute-start.4 = (bf16[800,256]{1,0:T(8,128)(2,1)}, bf16[800,256]{1,0:T(8,128)(2,1)S(1)}, u32[]{:S(2)}, u32[]{:S(2)}) collective-permute-start(bf16[800,256]{1,0:T(8,128)(2,1)} %copy-done.5), channel_id=1, source_target_pairs={{0,8},{8,0},{16,24},{24,16},{1,9},{9,1},{17,25},{25,17},{2,10},{10... | collective-permute-start | bytes 1228808 | tf_op jit(solution)/shard_map/ppermute | solution.py:48
  42.2 1.0 collective-permute-start.5
  43.1 9.7 %collective-permute-done.8.other_scales = f32[400,10]{1,0:T(8,128)S(1)} collective-permute-done((f32[400,10]{1,0:T(8,128)S(1)}, f32[400,10]{1,0:T(8,128)S(1)}, u32[]{:S(2)}, u32[]{:S(2)}) %collective-permute-start.8) | collective-permute-done | bytes 16032 | tf_op jit(solution)/shard_map/ppermute | solution.py:48
  52.8 3.8 %collective-permute-start.6 = (bf16[800,256]{1,0:T(8,128)(2,1)S(1)}, bf16[800,256]{1,0:T(8,128)(2,1)S(1)}, u32[]{:S(2)}, u32[]{:S(2)}) collective-permute-start(bf16[800,256]{1,0:T(8,128)(2,1)S(1)} %get-tuple-element.37), channel_id=1, source_target_pairs={{0,24},{8,16},{16,8},{24,0},{1,25},{9,17},{17,9},{25,1},{2,26},{10... | collective-permute-start | bytes 1228808 | tf_op jit(solution)/shard_map/ppermute | solution.py:48
  56.7 6.7 %shard_map.85 = bf16[800,2560]{1,0:T(8,128)(2,1)S(1)} custom-call(s32[4]{0:T(128)S(1)} %pad_add_fusion.place, bf16[400,2560]{1,0:T(8,128)(2,1)S(1)} %copy-done.4, f32[400,10]{1,0:T(8,128)S(1)} %copy.12.scales, bf16[400,2560]{1,0:T(8,128)(2,1)} %collective-permute-done.7.other_codes, f32[400,10]{1,0:T(8,128)S(1)} %collective-permute-done.8.other_scales), custom_call_target="tpu_custom_call" | custom-call | flops 4096000 | bytes 12288000 | tf_op jit(solution)/shard_map/pallas_call | solution.py:53
  63.4 6.3 %collective-permute-done.6.refs_3_ = bf16[800,256]{1,0:T(8,128)(2,1)S(1)} collective-permute-done((bf16[800,256]{1,0:T(8,128)(2,1)S(1)}, bf16[800,256]{1,0:T(8,128)(2,1)S(1)}, u32[]{:S(2)}, u32[]{:S(2)}) %collective-permute-start.6) | collective-permute-done | bytes 409632 | tf_op jit(solution)/shard_map/ppermute | solution.py:48
  69.7 1.2 shard_map.86
  70.9 3.1 %convolution_convert_fusion = bf16[512,2560]{1,0:T(8,128)(2,1)S(1)} fusion(bf16[512,800]{1,0:T(8,128)(2,1)S(1)} %get-tuple-element.44, bf16[800,2560]{1,0:T(8,128)(2,1)S(1)} %shard_map.85), kind=kOutput, calls=%fused_computation.4 | convolution fusion | flops 2098462720 | bytes 7536640 | tf_op jit(solution)/shard_map/dot_general | solution.py:154
  74.0 0.6 collective-permute-start.9
  74.6 3.1 %convolution_convert_fusion.1 = bf16[512,2560]{1,0:T(8,128)(2,1)S(1)} fusion(bf16[512,800]{1,0:T(8,128)(2,1)S(1)} %get-tuple-element.42, bf16[800,2560]{1,0:T(8,128)(2,1)S(1)} %shard_map.85), kind=kOutput, calls=%fused_computation.5 | convolution fusion | flops 2098462720 | bytes 7536640 | tf_op jit(solution)/shard_map/dot_general | solution.py:154
  77.7 2.8 %pad_maximum_fusion = bf16[4,4,64,2560]{3,2,1,0:T(8,128)(2,1)S(1)} fusion(bf16[4,1,64,2560]{3,2,1,0:T(8,128)(2,1)S(1)} %bitcast.63, bf16[4,1,64,2560]{3,2,1,0:T(8,128)(2,1)S(1)} %bitcast.61, bf16[4,1,64,2560]{3,2,1,0:T(8,128)(2,1)} %bitcast.17, bf16[4,1,64,2560]{3,2,1,0:T(8,128)(2,1)S(1)} %copy-done.6), kind=kLoop, calls=%fused_computation | loop fusion | flops 7864320 | bytes 10485760 | tf_op jit(solution)/shard_map/stack | solution.py:209
  80.5 0.5 fusion.8
  81.0 1.3 convolution_convert_fusion.4
  82.3 9.3 %collective-permute-start.16 = (bf16[800,256]{1,0:T(8,128)(2,1)S(1)}, bf16[800,256]{1,0:T(8,128)(2,1)S(1)}, u32[]{:S(2)}, u32[]{:S(2)}) collective-permute-start(bf16[800,256]{1,0:T(8,128)(2,1)S(1)} %convolution_convert_fusion.4), channel_id=1, source_target_pairs={{0,8},{8,0},{16,24},{24,16},{1,9},{9,1},{17,25},{25,17},{2,10},{10... | collective-permute-start | bytes 1228808 | tf_op jit(solution)/shard_map/ppermute | solution.py:48
  91.6 1.2 convolution_convert_fusion.3
  92.9 1.1 collective-permute-start.17
  93.9 0.7 convert_add_fusion
  94.7 0.1 slice.73
  94.8 0.6 collective-permute-start.10
  95.4 1.3 convolution_convert_fusion.2
  96.6 1.5 collective-permute-start.18
  98.2 2.3 %fusion.1 = bf16[400,2560]{1,0:T(8,128)(2,1)S(1)} fusion(bf16[400,1024]{1,0:T(8,128)(2,1)S(1)} %get-tuple-element.49, bf16[1024,2560]{1,0:T(8,128)(2,1)S(1)} %bitcast.58), kind=kOutput, calls=%fused_computation.7 | convolution fusion | flops 2099200000 | bytes 8110080 | tf_op jit(solution)/shard_map/dot_general | solution.py:154
  100.5 1.6 collective-permute-start.19
  102.0 1.3 convolution_convert_fusion.5.refs_0_
  103.3 5.3 %collective-permute-done.16.refs_1_ = bf16[800,256]{1,0:T(8,128)(2,1)S(1)} collective-permute-done((bf16[800,256]{1,0:T(8,128)(2,1)S(1)}, bf16[800,256]{1,0:T(8,128)(2,1)S(1)}, u32[]{:S(2)}, u32[]{:S(2)}) %collective-permute-start.16) | collective-permute-done | bytes 409632 | tf_op jit(solution)/shard_map/ppermute | solution.py:48
  108.6 15.2 %collective-permute-done.17.refs_2_ = bf16[800,256]{1,0:T(8,128)(2,1)S(1)} collective-permute-done((bf16[800,256]{1,0:T(8,128)(2,1)S(1)}, bf16[800,256]{1,0:T(8,128)(2,1)S(1)}, u32[]{:S(2)}, u32[]{:S(2)}) %collective-permute-start.17) | collective-permute-done | bytes 409632 | tf_op jit(solution)/shard_map/ppermute | solution.py:48
  123.8 5.7 %shard_map.87 = (bf16[256,3200]{1,0:T(8,128)(2,1)}, bf16[256,3200]{1,0:T(8,128)(2,1)}) custom-call(s32[4]{0:T(128)S(1)} %pad_add_fusion.place, bf16[256,3200]{1,0:T(8,128)(2,1)S(1)} %copy-done.1, bf16[256,3200]{1,0:T(8,128)(2,1)S(1)} %copy-done.3, bf16[800,256]{1,0:T(8,128)(2,1)S(1)} %convolution_convert_fusion.5.refs_0_, ...), custom_call_target="tpu_custom_call" | custom-call | flops 19660800 | bytes 8192000 | tf_op jit(solution)/shard_map/pallas_call | solution.py:53
  129.4 0.2 slice.50
  129.6 0.5 fusion.7
  130.2 2.5 %collective-permute-start.13 = (bf16[64,2560]{1,0:T(8,128)(2,1)S(1)}, bf16[64,2560]{1,0:T(8,128)(2,1)S(1)}, u32[]{:S(2)}, u32[]{:S(2)}) collective-permute-start(bf16[64,2560]{1,0:T(8,128)(2,1)S(1)} %get-tuple-element.59), channel_id=1, source_target_pairs={{0,24},{8,16},{16,8},{24,0},{1,25},{9,17},{17,9},{25,1},{2,26},{10... | collective-permute-start | bytes 983048 | tf_op jit(solution)/shard_map/ppermute | solution.py:48
  132.7 7.2 %collective-permute-start.12 = (bf16[64,2560]{1,0:T(8,128)(2,1)S(1)}, bf16[64,2560]{1,0:T(8,128)(2,1)S(1)}, u32[]{:S(2)}, u32[]{:S(2)}) collective-permute-start(bf16[64,2560]{1,0:T(8,128)(2,1)S(1)} %get-tuple-element.60), channel_id=1, source_target_pairs={{0,16},{8,24},{16,0},{24,8},{1,17},{9,25},{17,1},{25,9},{2,18},{10... | collective-permute-start | bytes 983048 | tf_op jit(solution)/shard_map/ppermute | solution.py:48
  139.9 6.3 %collective-permute-done.19 = bf16[400,2560]{1,0:T(8,128)(2,1)S(1)} collective-permute-done((bf16[400,2560]{1,0:T(8,128)(2,1)S(1)}, bf16[400,2560]{1,0:T(8,128)(2,1)S(1)}, u32[]{:S(2)}, u32[]{:S(2)}) %collective-permute-start.19) | collective-permute-done | bytes 2048032 | tf_op jit(solution)/shard_map/ppermute | solution.py:48
  146.2 4.3 %fusion = f32[400,2560]{1,0:T(8,128)} fusion(bf16[400,1024]{1,0:T(8,128)(2,1)S(1)} %get-tuple-element.48, bf16[1024,2560]{1,0:T(8,128)(2,1)S(1)} %bitcast.59, bf16[400,2560]{1,0:T(8,128)(2,1)S(1)} %collective-permute-done.19), kind=kOutput, calls=%fused_computation.6 | convolution fusion | flops 2100224000 | bytes 12206080 | tf_op jit(solution)/shard_map/dot_general | solution.py:154
  150.5 10.0 %collective-permute-done.12 = bf16[64,2560]{1,0:T(8,128)(2,1)S(1)} collective-permute-done((bf16[64,2560]{1,0:T(8,128)(2,1)S(1)}, bf16[64,2560]{1,0:T(8,128)(2,1)S(1)}, u32[]{:S(2)}, u32[]{:S(2)}) %collective-permute-start.12) | collective-permute-done | bytes 327712 | tf_op jit(solution)/shard_map/ppermute | solution.py:48
  160.5 0.9 fusion.5
  (33 shorter events, 0.3 us)
Async XLA Ops:
  0.6 56.0 %collective-permute-start.7 = (bf16[400,2560]{1,0:T(8,128)(2,1)}, bf16[400,2560]{1,0:T(8,128)(2,1)}, u32[]{:S(2)}, u32[]{:S(2)}) collective-permute-start(bf16[400,2560]{1,0:T(8,128)(2,1)} %codes.1), channel_id=1, source_target_pairs={{0,4},{4,0},{1,5},{5,1},{2,6},{6,2},{3,7},{7,3},{8,12},{12,8},{9,1... | collective-permute-start | bytes 6144008 | tf_op jit(solution)/shard_map/ppermute | solution.py:48
  3.6 15.6 %collective-permute-start = (bf16[64,2560]{1,0:T(8,128)(2,1)}, bf16[64,2560]{1,0:T(8,128)(2,1)}, u32[]{:S(2)}, u32[]{:S(2)}) collective-permute-start(bf16[64,2560]{1,0:T(8,128)(2,1)} %param.9), channel_id=1, source_target_pairs={{0,8},{8,0},{16,24},{24,16},{1,9},{9,1},{17,25},{25,17},{2,10},{10... | collective-permute-start | bytes 983048 | tf_op jit(solution)/shard_map/ppermute | solution.py:48
  5.2 25.9 %collective-permute-start.1 = (bf16[64,2560]{1,0:T(8,128)(2,1)}, bf16[64,2560]{1,0:T(8,128)(2,1)}, u32[]{:S(2)}, u32[]{:S(2)}) collective-permute-start(bf16[64,2560]{1,0:T(8,128)(2,1)} %param.9), channel_id=1, source_target_pairs={{0,16},{8,24},{16,0},{24,8},{1,17},{9,25},{17,1},{25,9},{2,18},{10... | collective-permute-start | bytes 983048 | tf_op jit(solution)/shard_map/ppermute | solution.py:48
  7.8 23.3 %collective-permute-start.2 = (bf16[64,2560]{1,0:T(8,128)(2,1)}, bf16[64,2560]{1,0:T(8,128)(2,1)}, u32[]{:S(2)}, u32[]{:S(2)}) collective-permute-start(bf16[64,2560]{1,0:T(8,128)(2,1)} %param.9), channel_id=1, source_target_pairs={{0,24},{8,16},{16,8},{24,0},{1,25},{9,17},{17,9},{25,1},{2,26},{10... | collective-permute-start | bytes 983048 | tf_op jit(solution)/shard_map/ppermute | solution.py:48
  8.1 1.4 copy-start
  9.5 1.4 copy-start.2
  11.0 20.2 %copy-start.7 = (bf16[64,2560]{1,0:T(8,128)(2,1)S(1)}, bf16[64,2560]{1,0:T(8,128)(2,1)}, u32[]{:S(2)}) copy-start(bf16[64,2560]{1,0:T(8,128)(2,1)} %param.9) | copy-start | bytes 983044
  13.8 20.2 %copy-start.5 = (bf16[800,256]{1,0:T(8,128)(2,1)}, bf16[800,256]{1,0:T(8,128)(2,1)S(1)}, u32[]{:S(2)}) copy-start(bf16[800,256]{1,0:T(8,128)(2,1)S(1)} %get-tuple-element.35) | copy-start | bytes 1228804
  13.8 21.7 %copy-start.8 = (f32[400,10]{0,1:T(8,128)S(1)}, f32[400,10]{0,1:T(8,128)}, u32[]{:S(2)}) copy-start(f32[400,10]{0,1:T(8,128)} %param.8) | copy-start | bytes 48004
  13.8 42.8 %copy-start.4 = (bf16[400,2560]{1,0:T(8,128)(2,1)S(1)}, bf16[400,2560]{1,0:T(8,128)(2,1)}, u32[]{:S(2)}) copy-start(bf16[400,2560]{1,0:T(8,128)(2,1)} %codes.1) | copy-start | bytes 6144004
  34.0 35.7 %collective-permute-start.3 = (bf16[4,64,2560]{2,1,0:T(8,128)(2,1)}, bf16[4,64,2560]{2,1,0:T(8,128)(2,1)}, u32[]{:S(2)}, u32[]{:S(2)}) collective-permute-start(bf16[4,64,2560]{2,1,0:T(8,128)(2,1)} %get-tuple-element.57), channel_id=1, source_target_pairs={{0,2},{2,0},{1,3},{3,1},{4,6},{6,4},{5,7},{7,5},{8,10},{10,8},{9,1... | collective-permute-start | bytes 3932168 | tf_op jit(solution)/shard_map/ppermute | solution.py:48
  35.7 17.1 %collective-permute-start.8 = (f32[400,10]{1,0:T(8,128)S(1)}, f32[400,10]{1,0:T(8,128)S(1)}, u32[]{:S(2)}, u32[]{:S(2)}) collective-permute-start(f32[400,10]{1,0:T(8,128)S(1)} %copy.12.scales), channel_id=1, source_target_pairs={{0,4},{4,0},{1,5},{5,1},{2,6},{6,2},{3,7},{7,3},{8,12},{12,8},{9,1... | collective-permute-start | bytes 48008 | tf_op jit(solution)/shard_map/ppermute | solution.py:48
  36.3 27.1 %collective-permute-start.4 = (bf16[800,256]{1,0:T(8,128)(2,1)}, bf16[800,256]{1,0:T(8,128)(2,1)S(1)}, u32[]{:S(2)}, u32[]{:S(2)}) collective-permute-start(bf16[800,256]{1,0:T(8,128)(2,1)} %copy-done.5), channel_id=1, source_target_pairs={{0,8},{8,0},{16,24},{24,16},{1,9},{9,1},{17,25},{25,17},{2,10},{10... | collective-permute-start | bytes 1228808 | tf_op jit(solution)/shard_map/ppermute | solution.py:48
  42.2 21.2 %collective-permute-start.5 = (bf16[800,256]{1,0:T(8,128)(2,1)S(1)}, bf16[800,256]{1,0:T(8,128)(2,1)S(1)}, u32[]{:S(2)}, u32[]{:S(2)}) collective-permute-start(bf16[800,256]{1,0:T(8,128)(2,1)S(1)} %get-tuple-element.36), channel_id=1, source_target_pairs={{0,16},{8,24},{16,0},{24,8},{1,17},{9,25},{17,1},{25,9},{2,18},{10... | collective-permute-start | bytes 1228808 | tf_op jit(solution)/shard_map/ppermute | solution.py:48
  52.8 16.8 %collective-permute-start.6 = (bf16[800,256]{1,0:T(8,128)(2,1)S(1)}, bf16[800,256]{1,0:T(8,128)(2,1)S(1)}, u32[]{:S(2)}, u32[]{:S(2)}) collective-permute-start(bf16[800,256]{1,0:T(8,128)(2,1)S(1)} %get-tuple-element.37), channel_id=1, source_target_pairs={{0,24},{8,16},{16,8},{24,0},{1,25},{9,17},{17,9},{25,1},{2,26},{10... | collective-permute-start | bytes 1228808 | tf_op jit(solution)/shard_map/ppermute | solution.py:48
  56.7 21.0 %collective-permute-start.14 = (bf16[4,64,2560]{2,1,0:T(8,128)(2,1)}, bf16[4,64,2560]{2,1,0:T(8,128)(2,1)S(1)}, u32[]{:S(2)}, u32[]{:S(2)}) collective-permute-start(bf16[4,64,2560]{2,1,0:T(8,128)(2,1)} %get-tuple-element.57), channel_id=1, source_target_pairs={{0,1},{1,0},{2,3},{3,2},{4,5},{5,4},{6,7},{7,6},{8,9},{9,8},{10,11... | collective-permute-start | bytes 3932168 | tf_op jit(solution)/shard_map/ppermute | solution.py:48
  69.7 8.0 %collective-permute-start.15 = (bf16[4,64,2560]{2,1,0:T(8,128)(2,1)}, bf16[4,64,2560]{2,1,0:T(8,128)(2,1)S(1)}, u32[]{:S(2)}, u32[]{:S(2)}) collective-permute-start(bf16[4,64,2560]{2,1,0:T(8,128)(2,1)} %collective-permute-done.3), channel_id=1, source_target_pairs={{0,1},{1,0},{2,3},{3,2},{4,5},{5,4},{6,7},{7,6},{8,9},{9,8},{10,11... | collective-permute-start | bytes 3932168 | tf_op jit(solution)/shard_map/ppermute | solution.py:48
  74.0 19.9 %collective-permute-start.9 = (bf16[512,2560]{1,0:T(8,128)(2,1)S(1)}, bf16[512,2560]{1,0:T(8,128)(2,1)S(1)}, u32[]{:S(2)}, u32[]{:S(2)}) collective-permute-start(bf16[512,2560]{1,0:T(8,128)(2,1)S(1)} %convolution_convert_fusion), channel_id=1, source_target_pairs={{0,1},{1,0},{2,3},{3,2},{4,5},{5,4},{6,7},{7,6},{8,9},{9,8},{10,11... | collective-permute-start | bytes 7864328 | tf_op jit(solution)/shard_map/ppermute | solution.py:48
  74.6 3.1 %copy-start.6 = (bf16[4,1,64,2560]{3,2,1,0:T(8,128)(2,1)S(1)}, bf16[4,1,64,2560]{3,2,1,0:T(8,128)(2,1)}, u32[]{:S(2)}) copy-start(bf16[4,1,64,2560]{3,2,1,0:T(8,128)(2,1)} %get-tuple-element.56) | copy-start | bytes 3932164
  82.3 26.3 %collective-permute-start.16 = (bf16[800,256]{1,0:T(8,128)(2,1)S(1)}, bf16[800,256]{1,0:T(8,128)(2,1)S(1)}, u32[]{:S(2)}, u32[]{:S(2)}) collective-permute-start(bf16[800,256]{1,0:T(8,128)(2,1)S(1)} %convolution_convert_fusion.4), channel_id=1, source_target_pairs={{0,8},{8,0},{16,24},{24,16},{1,9},{9,1},{17,25},{25,17},{2,10},{10... | collective-permute-start | bytes 1228808 | tf_op jit(solution)/shard_map/ppermute | solution.py:48
  92.9 30.9 %collective-permute-start.17 = (bf16[800,256]{1,0:T(8,128)(2,1)S(1)}, bf16[800,256]{1,0:T(8,128)(2,1)S(1)}, u32[]{:S(2)}, u32[]{:S(2)}) collective-permute-start(bf16[800,256]{1,0:T(8,128)(2,1)S(1)} %convolution_convert_fusion.3), channel_id=1, source_target_pairs={{0,16},{8,24},{16,0},{24,8},{1,17},{9,25},{17,1},{25,9},{2,18},{10... | collective-permute-start | bytes 1228808 | tf_op jit(solution)/shard_map/ppermute | solution.py:48
  94.8 34.8 %collective-permute-start.10 = (bf16[4,64,2560]{2,1,0:T(8,128)(2,1)S(1)}, bf16[4,64,2560]{2,1,0:T(8,128)(2,1)S(1)}, u32[]{:S(2)}, u32[]{:S(2)}) collective-permute-start(bf16[4,64,2560]{2,1,0:T(8,128)(2,1)S(1)} %bitcast.67), channel_id=1, source_target_pairs={{0,2},{2,0},{1,3},{3,1},{4,6},{6,4},{5,7},{7,5},{8,10},{10,8},{9,1... | collective-permute-start | bytes 3932168 | tf_op jit(solution)/shard_map/ppermute | solution.py:48
  96.6 27.1 %collective-permute-start.18 = (bf16[800,256]{1,0:T(8,128)(2,1)S(1)}, bf16[800,256]{1,0:T(8,128)(2,1)S(1)}, u32[]{:S(2)}, u32[]{:S(2)}) collective-permute-start(bf16[800,256]{1,0:T(8,128)(2,1)S(1)} %convolution_convert_fusion.2), channel_id=1, source_target_pairs={{0,24},{8,16},{16,8},{24,0},{1,25},{9,17},{17,9},{25,1},{2,26},{10... | collective-permute-start | bytes 1228808 | tf_op jit(solution)/shard_map/ppermute | solution.py:48
  100.5 45.8 %collective-permute-start.19 = (bf16[400,2560]{1,0:T(8,128)(2,1)S(1)}, bf16[400,2560]{1,0:T(8,128)(2,1)S(1)}, u32[]{:S(2)}, u32[]{:S(2)}) collective-permute-start(bf16[400,2560]{1,0:T(8,128)(2,1)S(1)} %fusion.1), channel_id=1, source_target_pairs={{0,4},{4,0},{1,5},{5,1},{2,6},{6,2},{3,7},{7,3},{8,12},{12,8},{9,1... | collective-permute-start | bytes 6144008 | tf_op jit(solution)/shard_map/ppermute | solution.py:48
  102.0 21.7 %copy-start.1 = (bf16[256,3200]{1,0:T(8,128)(2,1)S(1)}, bf16[256,3200]{1,0:T(8,128)(2,1)}, u32[]{:S(2)}) copy-start(bf16[256,3200]{1,0:T(8,128)(2,1)} %gate.3) | copy-start | bytes 4915204
  102.0 21.7 %copy-start.3 = (bf16[256,3200]{1,0:T(8,128)(2,1)S(1)}, bf16[256,3200]{1,0:T(8,128)(2,1)}, u32[]{:S(2)}) copy-start(bf16[256,3200]{1,0:T(8,128)(2,1)} %up.3) | copy-start | bytes 4915204
  130.2 20.3 %collective-permute-start.13 = (bf16[64,2560]{1,0:T(8,128)(2,1)S(1)}, bf16[64,2560]{1,0:T(8,128)(2,1)S(1)}, u32[]{:S(2)}, u32[]{:S(2)}) collective-permute-start(bf16[64,2560]{1,0:T(8,128)(2,1)S(1)} %get-tuple-element.59), channel_id=1, source_target_pairs={{0,24},{8,16},{16,8},{24,0},{1,25},{9,17},{17,9},{25,1},{2,26},{10... | collective-permute-start | bytes 983048 | tf_op jit(solution)/shard_map/ppermute | solution.py:48
  132.7 27.8 %collective-permute-start.12 = (bf16[64,2560]{1,0:T(8,128)(2,1)S(1)}, bf16[64,2560]{1,0:T(8,128)(2,1)S(1)}, u32[]{:S(2)}, u32[]{:S(2)}) collective-permute-start(bf16[64,2560]{1,0:T(8,128)(2,1)S(1)} %get-tuple-element.60), channel_id=1, source_target_pairs={{0,16},{8,24},{16,0},{24,8},{1,17},{9,25},{17,1},{25,9},{2,18},{10... | collective-permute-start | bytes 983048 | tf_op jit(solution)/shard_map/ppermute | solution.py:48
  139.9 20.6 %collective-permute-start.11 = (bf16[64,2560]{1,0:T(8,128)(2,1)S(1)}, bf16[64,2560]{1,0:T(8,128)(2,1)S(1)}, u32[]{:S(2)}, u32[]{:S(2)}) collective-permute-start(bf16[64,2560]{1,0:T(8,128)(2,1)S(1)} %get-tuple-element.58), channel_id=1, source_target_pairs={{0,8},{8,0},{16,24},{24,16},{1,9},{9,1},{17,25},{25,17},{2,10},{10... | collective-permute-start | bytes 983048 | tf_op jit(solution)/shard_map/ppermute | solution.py:48

commit v3 on v2

--- a/solution.py
+++ b/solution.py
@@ -8,7 +8,6 @@
 from jax.sharding import Mesh, PartitionSpec as P
 
 VMEM_BYTES = 32 * 2**20
-WEIGHT_COST = 6
 
 
 def dequantize(codes, scales):
@@ -75,8 +74,8 @@
     return pl.multiple_of(((place[2] ^ (block % 2)) * 2 + (place[3] ^ (block // 2))) * rows, 16)
 
 
-def hidden_kernel(nz, units, place, gate, up, *refs):
-    outs, (natural, columns) = refs[:nz], refs[nz:]
+def hidden_kernel(parts, units, place, gate, up, *refs):
+    outs, (natural, columns) = refs[: len(parts)], refs[len(parts) :]
     step = pl.program_id(0)
     group, span = gate.shape
     rows = group // 4
@@ -89,35 +88,48 @@
     @pl.when(step == pl.num_programs(0) - 1)
     def _():
         half = units // 2
-        for k in range(nz):
-            for r in range(2):
-                start = (place[0] ^ k) * units + (place[1] ^ r) * half
-                outs[k][r * half : (r + 1) * half, :] = columns[
+        for out, (k, first, count) in zip(outs, parts):
+            for r in range(count):
+                start = (place[0] ^ k) * units + (place[1] ^ (first + r)) * half
+                out[r * half : (r + 1) * half, :] = columns[
                     pl.ds(pl.multiple_of(start, 16), half), :
                 ]
 
 
-def weight_kernel(place, codes, scales, other_codes, other_scales, weight):
-    lane = lax.broadcasted_iota(jnp.int32, scales.shape, 1)
-    half = codes.shape[0]
-    for r, (code, scale) in enumerate(((codes, scales), (other_codes, other_scales))):
-        mine = jnp.where(lane == pl.program_id(0), scale[...], 0.0)
-        value = code[...].astype(jnp.float32) * jnp.sum(mine, axis=1, keepdims=True)
-        weight[r * half : (r + 1) * half, :] = value.astype(jnp.bfloat16)
-
-
-def columns_kernel(nz, place, *refs):
-    pieces, (keep, send, mine, theirs) = refs[:nz], refs[nz:]
-    half, group = mine.shape[0], pieces[0].shape[1]
+def weight_kernel(place, codes, scales, *halves):
+    span = codes.shape[1] // scales.shape[1]
+    per_half = scales.shape[1] // 2
+    for block in range(scales.shape[1]):
+        value = codes[:, block * span : (block + 1) * span].astype(jnp.float32)
+        value = (value * scales[:, block : block + 1]).astype(jnp.bfloat16)
+        at = block % per_half * span
+        halves[block // per_half][:, at : at + span] = value
+
+
+def join_kernel(place, own_a, own_b, other_a, other_b, weight):
+    half, middle = own_a.shape
+    weight[:half, :middle] = own_a[...]
+    weight[:half, middle:] = own_b[...]
+    weight[half:, :middle] = other_a[...]
+    weight[half:, middle:] = other_b[...]
+
+
+def columns_kernel(parts, by_rows, by_lanes, place, *refs):
+    pieces, (keep, send, *rest) = refs[: len(parts)], refs[len(parts) :]
+    half, group = rest[0].shape[0], pieces[0].shape[1]
     rows = group // 4
-    for k in range(nz):
-        turned = pieces[k][...].T
+    for piece, (k, first, count) in zip(pieces, parts):
+        turned = piece[...].T
+        row, lane = by_rows.index(k), by_lanes.index(k)
+        lanes = slice(lane % 2 * group, (lane % 2 + 1) * group)
         for b in range(4):
             target = send if b >= 2 else keep
-            start = ((b % 2) * nz + k) * rows
-            target[start : start + rows, :] = turned[b * rows : (b + 1) * rows, :]
-        mine[:, k * group : (k + 1) * group] = pieces[k][:half, :]
-        theirs[:, k * group : (k + 1) * group] = pieces[k][half:, :]
+            start = ((b % 2) * len(by_rows) + row) * rows
+            target[start : start + rows, first * half : (first + count) * half] = turned[
+                b * rows : (b + 1) * rows, :
+            ]
+        for r in range(count):
+            rest[lane // 2 * 2 + first + r][:, lanes] = piece[r * half : (r + 1) * half, :]
 
 
 def grads_kernel(nz, units, place, gate, up, *refs):
@@ -157,76 +169,117 @@
 def paired_body(gate_pre, up_pre, down_codes, down_scales, cotangent):
     group_rows, local_hidden = gate_pre.shape
     owned, width = down_codes.shape
-    nz = lax.axis_size("z")
     rows = cotangent.shape[0]
-    units = 2 * owned
+    nz, units, middle = 4, 2 * owned, width // 2
     total_tokens = group_rows * nz * 2
     bf16, f32 = jnp.bfloat16, jnp.float32
     place = jnp.stack([lax.axis_index(name) for name in ("z", "x", "y", "c")]).astype(jnp.int32)
     struct = jax.ShapeDtypeStruct
-
-    other_codes, other_scales = exchange(down_codes, "x", 1), exchange(down_scales, "x", 1)
-
+    barrier = lax.optimization_barrier
+
+    far = exchange(cotangent, "z", 2)
+
+    own_a, own_b = call_kernel(
+        weight_kernel, place, (down_codes, down_scales),
+        [whole(down_codes.shape), whole(down_scales.shape)],
+        [struct((owned, middle), bf16)] * 2, [whole((owned, middle))] * 2, (1,), [],
+        (2 * owned * width, 4 * owned * width, 0),
+    )
+    other_a = exchange(own_a, "x", 1)
+
+    parts = ((0, 0, 2), (1, 0, 2), (2, 0, 1), (3, 0, 1), (2, 1, 1), (3, 1, 1))
+    pieces = [struct((count * owned, group_rows), bf16) for _, _, count in parts]
+    piece_specs = [whole(piece.shape) for piece in pieces]
     span = column_span(local_hidden)
     steps = local_hidden // span
-    piece = struct((units, group_rows), bf16)
     wide = pl.BlockSpec((group_rows, span), lambda i, place: (0, i))
     act_bytes = group_rows * local_hidden * 2
     act_scratch = [pltpu.VMEM((group_rows, span), bf16), pltpu.VMEM((local_hidden, group_rows), bf16)]
     sent = call_kernel(
-        functools.partial(hidden_kernel, nz, units), place, (gate_pre, up_pre), [wide] * 2,
-        [piece] * nz, [whole(piece.shape)] * nz, (steps,), act_scratch,
+        functools.partial(hidden_kernel, parts, units), place, (gate_pre, up_pre), [wide] * 2,
+        pieces, piece_specs, (steps,), act_scratch,
         (4 * act_bytes, 3 * act_bytes, act_bytes // 2),
     )
 
-    line = [exchange(cotangent, "z", k) for k in range(1, nz)]
-    line, sent = lax.optimization_barrier((line, sent))
-    line = jnp.stack([cotangent] + line)
-    columns = [sent[0]] + [exchange(sent[k], "z", k) for k in range(1, nz)]
-    over_y = exchange(line, "y", 1)
-    other_core = exchange(line, "c", 1)
-
-    nblocks = down_scales.shape[1]
-    block = width // nblocks
-    code_block = pl.BlockSpec((owned, block), lambda i, place: (0, i))
+    far, sent = barrier((far, sent))
+    even = jnp.stack([cotangent, far])
+    odd = exchange(even, "z", 1)
+    even_y = exchange(even, "y", 1)
+    columns = [sent[0], None] + [exchange(sent[i], "z", parts[i][0]) for i in (2, 3)]
+    odd, even_y, columns, other_a, sent, own_b = barrier((odd, even_y, columns, other_a, sent, own_b))
+
+    odd_y = exchange(odd, "y", 1)
+    other_b = exchange(own_b, "x", 1)
+    columns[1] = exchange(sent[1], "z", 1)
+    columns += [exchange(sent[i], "z", parts[i][0]) for i in (4, 5)]
+    even_c = [even, even_y, exchange(even, "c", 1), exchange(even_y, "c", 1)]
+    odd_c = exchange(odd, "c", 1)
+    odd_y, columns, other_b = barrier((odd_y, columns, other_b))
+    tile = column_span(middle)
     weight = call_kernel(
-        weight_kernel, place, (down_codes, down_scales, other_codes, other_scales),
-        [code_block, whole(down_scales.shape)] * 2, struct((units, width), bf16),
-        pl.BlockSpec((units, block), lambda i, place: (0, i)), (nblocks,), [],
-        (2 * units * width, WEIGHT_COST * units * width, 0),
-    )
-    over_y, columns, weight = lax.optimization_barrier((over_y, columns, weight))
-    received = (line, over_y, other_core, exchange(over_y, "c", 1))
+        join_kernel, place, (own_a, own_b, other_a, other_b), [whole((owned, middle))] * 4,
+        struct((units, width), bf16), whole((units, width)), (1,), [],
+        (0, 4 * units * width, 0),
+    )
+
     half_tokens = nz * group_rows // 2
-    keep, send, mine, theirs = call_kernel(
-        functools.partial(columns_kernel, nz), place, tuple(columns),
-        [whole(piece.shape)] * nz,
-        [struct((half_tokens, units), bf16)] * 2 + [struct((owned, 2 * half_tokens), bf16)] * 2,
-        [whole((half_tokens, units))] * 2 + [whole((owned, 2 * half_tokens))] * 2, (1,), [],
+    by_rows, by_lanes = (1, 3, 0, 2), (0, 2, 1, 3)
+    keep, send, *by_units = call_kernel(
+        functools.partial(columns_kernel, parts, by_rows, by_lanes), place, columns, piece_specs,
+        [struct((half_tokens, units), bf16)] * 2 + [struct((owned, half_tokens), bf16)] * 4,
+        [whole((half_tokens, units))] * 2 + [whole((owned, half_tokens))] * 4, (1,), [],
         (0, 12 * units * half_tokens, 0),
     )
 
-    tokens = jnp.stack(received, axis=1).reshape(nz, group_rows, width)
-    back = [matmul(weight, tokens[k], 1, 1, bf16) for k in range(nz)]
-    back = [back[0]] + [exchange(back[k], "z", k) for k in range(1, nz)]
-
-    tokens = tokens.reshape(-1, width)
+    odd_c = [odd, odd_y, odd_c, exchange(odd_y, "c", 1)]
+    even_c, odd_c, send, keep = barrier((even_c, odd_c, send, keep))
+    tokens = [jnp.stack(c, axis=1).reshape(2, group_rows, width) for c in (even_c, odd_c)]
+
     factor = float(total_tokens) ** (-0.5)
-    over_x = exchange((matmul(theirs, tokens) * factor).astype(bf16), "x", 1)
-    weight_grad = matmul(mine, tokens) * factor + over_x.astype(f32)
-
+    flat = [t.reshape(half_tokens, width) for t in tokens]
+
+    first_units, first_rows = units // 48 * 16, owned // 48 * 16
+
+    def grad_half(r, low, high):
+        near, far = by_units[r][low:high], by_units[2 + r][low:high]
+        return (matmul(near, flat[0]) + matmul(far, flat[1])) * factor
+
+    def back_of(k, low, high):
+        return matmul(weight[low:high], tokens[k % 2][k // 2], 1, 1, bf16)
+
+    far_first = [back_of(k, 0, first_units) for k in (2, 3)]
+    far_last = [back_of(k, first_units, units) for k in (2, 3)]
+    far_first, far_last, flat = barrier((far_first, far_last, flat))
+    theirs = grad_half(1, 0, first_rows).astype(bf16), grad_half(1, first_rows, owned).astype(bf16)
+    theirs, send, keep = barrier((theirs, send, keep))
+    far_first = [exchange(value, "z", 2 + i) for i, value in enumerate(far_first)]
+    over_x = [exchange(theirs[0], "x", 1)]
     over_c = exchange(matmul(send, weight, dtype=bf16), "c", 1)
     own_c = matmul(keep, weight, dtype=bf16)
+    own_c, over_c, tokens = barrier((own_c, over_c, tokens))
+    near_back = [back_of(0, 0, units), back_of(1, 0, units)]
+    far_first, over_x, far_last, theirs, own_c, over_c = barrier(
+        (far_first, over_x, far_last, theirs, own_c, over_c)
+    )
+    back = [near_back[0], exchange(near_back[1], "z", 1)]
+    back += [
+        jnp.concatenate([value, exchange(far_last[i], "z", 2 + i)])
+        for i, value in enumerate(far_first)
+    ]
+    over_x.append(exchange(theirs[1], "x", 1))
+
     sums = (own_c.astype(f32) + over_c.astype(f32)).reshape(2, nz, rows, width)
-    over_y = sums[0] + exchange(sums[1].astype(bf16), "y", 1).astype(f32)
-    layer_out = over_y[0]
-    for k in range(1, nz):
-        layer_out = layer_out + exchange(over_y[k].astype(bf16), "z", k).astype(f32)
-    layer_out = layer_out.astype(bf16)
-
+    odd_sum = sums[0, :2] + exchange(sums[1, :2].astype(bf16), "y", 1).astype(f32)
+    even_sum = sums[0, 2:] + exchange(sums[1, 2:].astype(bf16), "y", 1).astype(f32)
+    near = exchange(odd_sum.astype(bf16), "z", 1).astype(f32)
+    ours, across = even_sum[0] + near[0], (even_sum[1] + near[1]).astype(bf16)
+    layer_out = (ours + exchange(across, "z", 2).astype(f32)).astype(bf16)
+
+    weight_grad = grad_half(0, 0, owned) + jnp.concatenate(over_x).astype(f32)
+    back, _ = barrier((back, across))
     gate_grad, up_grad = call_kernel(
         functools.partial(grads_kernel, nz, units), place, (gate_pre, up_pre, *back),
-        [wide] * 2 + [whole(piece.shape)] * nz,
+        [wide] * 2 + [whole((units, group_rows))] * nz,
         [struct((group_rows, local_hidden), bf16)] * 2, [wide] * 2, (steps,), act_scratch[::-1],
         (12 * act_bytes, 5 * act_bytes, act_bytes // 2),
     )
@@ -307,11 +360,12 @@
         layer = P(("z", "x", "y", "c"), None)
         owned = hidden // (dp * tensor)
         rows = tokens // (dp * tensor)
-        pairs = fine.shape["x"] == 2 and fine.shape["y"] == 2 and nz & (nz - 1) == 0
+        pairs = fine.shape["x"] == 2 and fine.shape["y"] == 2 and nz == 4
         aligned = owned % 16 == 0 and rows % 16 == 0 and column_span(hidden // tensor)
-        block = cotangent.shape[1] // down_scales.shape[1]
+        nblocks = down_scales.shape[1]
+        blocks = nblocks % 2 == 0 and cotangent.shape[1] // nblocks % 128 == 0
         return jax.shard_map(
-            paired_body if pairs and aligned and block % 128 == 0 else body,
+            paired_body if pairs and aligned and blocks else body,
             mesh=fine,
             in_specs=(act, act, weight, weight, layer),
             out_specs=(layer, act, act, weight),

time: 162 us -> 164 us (1.012)
  waiting for transfers between devices: 70 us -> 91.1 us
  starting transfers between devices: 44.6 us -> 33.5 us
  other arithmetic: 7.84 us -> 3.24 us
  Pallas kernels: 16.4 us -> 11.8 us
    ppermute x20 -> x27, waiting for transfers between devices: 70 us -> 91.1 us  [exchange(): return lax.ppermute(value, axis, [(i, i ^ offset) for i in range(size)])]
    ppermute x20 -> x27, starting transfers between devices: 44.6 us -> 33.5 us  [exchange(): return lax.ppermute(value, axis, [(i, i ^ offset) for i in range(size)])]
    another operation x3 -> x4, other arithmetic: 6.16 us -> 1.01 us  [the longest x2 0.66 us: paired_body(): jnp.stack(c, axis=1).reshape(2, group_rows, width)]
    pallas_call x4 -> x5, Pallas kernels: 16.4 us -> 11.8 us  [call_kernel(): pl.pallas_call(kernel, out_shape=out_shapes, grid_spec=pltpu.PrefetchScal...]
    dot_general x8 -> x14, matrix products: 17.8 us -> 19.2 us  [matmul(): lax.dot_general(lhs, rhs, dims, preferred_element_type=jnp.float32)]
    unnamed x19 -> x11, local copies, waits for them, and re-layouts: 3.03 us -> 3.9 us
  transfers between devices with their start and end apart: 20 -> 27, of which waited for: 8 -> 13; matrix products, arithmetic and copies ran while one was open for 16% -> 7% of each run, Pallas kernels for 10% -> 7%
where the time goes in v3:
time: 164 us
  waiting for transfers between devices  91.1 us (56%)
  starting transfers between devices  33.5 us (20%)
  matrix products  19.2 us (12%)
  Pallas kernels  11.8 us (7%)
  local copies, waits for them, and re-layouts  4.36 us (3%)
  other arithmetic  3.24 us (2%)
    ppermute x27, waiting for transfers between devices, exchange(): return lax.ppermute(value, axis, [(i, i ^ offset) for i in range(size)])  91.1 us
    ppermute x27, starting transfers between devices, exchange(): return lax.ppermute(value, axis, [(i, i ^ offset) for i in range(size)])  33.5 us
    dot_general x14, matrix products, matmul(): lax.dot_general(lhs, rhs, dims, preferred_element_type=jnp.float32)  19.2 us
    pallas_call x5, Pallas kernels, call_kernel(): pl.pallas_call(kernel, out_shape=out_shapes, grid_spec=pltpu.PrefetchScal...  11.8 us
    unnamed x11, local copies, waits for them, and re-layouts  3.9 us
  transfers between devices with their start and end apart: 27, of which 13 were waited for; matrix products, arithmetic and copies ran while one was open for 7% of the time, Pallas kernels for 7%

profile of v3, /device:TPU:0, one launch (start us, length us, event | category | flops | bytes accessed | tf_op | source)
XLA Modules:
  0.0 164.1 jit_solution(5738159283131834048)
XLA Ops:
  0.6 4.1 %collective-permute-start = (bf16[64,2560]{1,0:T(8,128)(2,1)}, bf16[64,2560]{1,0:T(8,128)(2,1)S(1)}, u32[]{:S(2)}, u32[]{:S(2)}) collective-permute-start(bf16[64,2560]{1,0:T(8,128)(2,1)} %param.9), channel_id=1, source_target_pairs={{0,16},{8,24},{16,0},{24,8},{1,17},{9,25},{17,1},{25,9},{2,18},{10... | collective-permute-start | bytes 983048 | tf_op jit(solution)/shard_map/ppermute | solution.py:47
  4.7 0.9 copy.10.scales
  5.7 1.6 copy-done.3
  7.3 1.1 shard_map.84
  8.4 1.6 collective-permute-start.5
  10.0 1.4 copy-done.1
  11.4 2.8 %shard_map.85 = (bf16[800,256]{1,0:T(8,128)(2,1)S(1)}, bf16[800,256]{1,0:T(8,128)(2,1)S(1)}, bf16[400,256]{1,0:T(8,128)(2,1)S(1)}, bf16[400,256]{1,0:T(8,128)(2,...) custom-call(s32[4]{0:T(128)S(1)} %pad_add_fusion.place, bf16[256,3200]{1,0:T(8,128)(2,1)S(1)} %copy-done, ...), custom_call_target="tpu_custom_call" | custom-call | flops 6553600 | bytes 4915200 | tf_op jit(solution)/shard_map/pallas_call | solution.py:52
  14.3 5.4 %collective-permute-done = bf16[64,2560]{1,0:T(8,128)(2,1)S(1)} collective-permute-done((bf16[64,2560]{1,0:T(8,128)(2,1)}, bf16[64,2560]{1,0:T(8,128)(2,1)S(1)}, u32[]{:S(2)}, u32[]{:S(2)}) %collective-permute-start) | collective-permute-done | bytes 327712 | tf_op jit(solution)/shard_map/ppermute | solution.py:47
  19.8 0.9 collective-permute-start.1
  20.6 1.5 collective-permute-start.2
  22.2 3.3 %collective-permute-start.3 = (bf16[400,256]{1,0:T(8,128)(2,1)S(1)}, bf16[400,256]{1,0:T(8,128)(2,1)S(1)}, u32[]{:S(2)}, u32[]{:S(2)}) collective-permute-start(bf16[400,256]{1,0:T(8,128)(2,1)S(1)} %get-tuple-element.90), channel_id=1, source_target_pairs={{0,16},{8,24},{16,0},{24,8},{1,17},{9,25},{17,1},{25,9},{2,18},{10... | collective-permute-start | bytes 614408 | tf_op jit(solution)/shard_map/ppermute | solution.py:47
  25.8 14.4 %collective-permute-done.3.refs_2_ = bf16[400,256]{1,0:T(8,128)(2,1)S(1)} collective-permute-done((bf16[400,256]{1,0:T(8,128)(2,1)S(1)}, bf16[400,256]{1,0:T(8,128)(2,1)S(1)}, u32[]{:S(2)}, u32[]{:S(2)}) %collective-permute-start.3) | collective-permute-done | bytes 204832 | tf_op jit(solution)/shard_map/ppermute | solution.py:47
  40.1 6.9 %collective-permute-done.4.refs_3_ = bf16[400,256]{1,0:T(8,128)(2,1)S(1)} collective-permute-done((bf16[400,256]{1,0:T(8,128)(2,1)S(1)}, bf16[400,256]{1,0:T(8,128)(2,1)S(1)}, u32[]{:S(2)}, u32[]{:S(2)}) %collective-permute-start.4) | collective-permute-done | bytes 204832 | tf_op jit(solution)/shard_map/ppermute | solution.py:47
  47.1 1.6 collective-permute-start.10
  48.6 1.5 collective-permute-start.6
  50.1 2.2 %collective-permute-start.8 = (bf16[400,256]{1,0:T(8,128)(2,1)S(1)}, bf16[400,256]{1,0:T(8,128)(2,1)S(1)}, u32[]{:S(2)}, u32[]{:S(2)}) collective-permute-start(bf16[400,256]{1,0:T(8,128)(2,1)S(1)} %get-tuple-element.103), channel_id=1, source_target_pairs={{0,16},{8,24},{16,0},{24,8},{1,17},{9,25},{17,1},{25,9},{2,18},{10... | collective-permute-start | bytes 614408 | tf_op jit(solution)/shard_map/ppermute | solution.py:47
  52.4 2.2 %collective-permute-start.9 = (bf16[400,256]{1,0:T(8,128)(2,1)S(1)}, bf16[400,256]{1,0:T(8,128)(2,1)S(1)}, u32[]{:S(2)}, u32[]{:S(2)}) collective-permute-start(bf16[400,256]{1,0:T(8,128)(2,1)S(1)} %get-tuple-element.104), channel_id=1, source_target_pairs={{0,24},{8,16},{16,8},{24,0},{1,25},{9,17},{17,9},{25,1},{2,26},{10... | collective-permute-start | bytes 614408 | tf_op jit(solution)/shard_map/ppermute | solution.py:47
  54.5 10.0 %collective-permute-done.8.refs_4_ = bf16[400,256]{1,0:T(8,128)(2,1)S(1)} collective-permute-done((bf16[400,256]{1,0:T(8,128)(2,1)S(1)}, bf16[400,256]{1,0:T(8,128)(2,1)S(1)}, u32[]{:S(2)}, u32[]{:S(2)}) %collective-permute-start.8) | collective-permute-done | bytes 204832 | tf_op jit(solution)/shard_map/ppermute | solution.py:47
  64.5 3.7 %collective-permute-done.9.refs_5_ = bf16[400,256]{1,0:T(8,128)(2,1)S(1)} collective-permute-done((bf16[400,256]{1,0:T(8,128)(2,1)S(1)}, bf16[400,256]{1,0:T(8,128)(2,1)S(1)}, u32[]{:S(2)}, u32[]{:S(2)}) %collective-permute-start.9) | collective-permute-done | bytes 204832 | tf_op jit(solution)/shard_map/ppermute | solution.py:47
  68.2 1.0 collective-permute-done.7.refs_1_
  69.2 1.9 %collective-permute-done.10.other_b = bf16[400,1280]{1,0:T(8,128)(2,1)S(1)} collective-permute-done((bf16[400,1280]{1,0:T(8,128)(2,1)S(1)}, bf16[400,1280]{1,0:T(8,128)(2,1)S(1)}, u32[]{:S(2)}, u32[]{:S(2)}) %collective-permute-start.10) | collective-permute-done | bytes 1024032 | tf_op jit(solution)/shard_map/ppermute | solution.py:47
  72.0 1.3 shard_map.87
  74.0 0.9 fusion.27
  75.9 0.9 fusion.24
  77.3 0.9 fusion.46
  78.7 0.9 fusion.2
  80.2 3.1 %convolution_convert_fusion = bf16[512,2560]{1,0:T(8,128)(2,1)S(1)} fusion(bf16[512,800]{1,0:T(8,128)(2,1)S(1)} %get-tuple-element.137, bf16[800,2560]{1,0:T(8,128)(2,1)S(1)} %shard_map.86), kind=kOutput, calls=%fused_computation.3 | convolution fusion | flops 2098462720 | bytes 7536640 | tf_op jit(solution)/shard_map/dot_general | solution.py:166
  83.9 1.5 collective-permute-start.17
  85.5 2.4 %collective-permute-start.16 = (bf16[256,256]{1,0:T(8,128)(2,1)S(1)}, bf16[256,256]{1,0:T(8,128)(2,1)S(1)}, u32[]{:S(2)}, u32[]{:S(2)}) collective-permute-start(bf16[256,256]{1,0:T(8,128)(2,1)S(1)} %fusion.37), channel_id=1, source_target_pairs={{0,24},{8,16},{16,8},{24,0},{1,25},{9,17},{17,9},{25,1},{2,26},{10... | collective-permute-start | bytes 393224 | tf_op jit(solution)/shard_map/ppermute | solution.py:47
  87.8 3.3 %convolution_convert_fusion.1 = bf16[512,2560]{1,0:T(8,128)(2,1)S(1)} fusion(bf16[512,800]{1,0:T(8,128)(2,1)S(1)} %get-tuple-element.136, bf16[800,2560]{1,0:T(8,128)(2,1)S(1)} %shard_map.86), kind=kOutput, calls=%fused_computation.4 | convolution fusion | flops 2098462720 | bytes 7536640 | tf_op jit(solution)/shard_map/dot_general | solution.py:166
  91.1 5.9 %collective-permute-done.15 = bf16[256,256]{1,0:T(8,128)(2,1)S(1)} collective-permute-done((bf16[256,256]{1,0:T(8,128)(2,1)S(1)}, bf16[256,256]{1,0:T(8,128)(2,1)S(1)}, u32[]{:S(2)}, u32[]{:S(2)}) %collective-permute-start.15) | collective-permute-done | bytes 131104 | tf_op jit(solution)/shard_map/ppermute | solution.py:47
  97.0 3.6 %collective-permute-done.17 = bf16[128,2560]{1,0:T(8,128)(2,1)S(1)} collective-permute-done((bf16[128,2560]{1,0:T(8,128)(2,1)S(1)}, bf16[128,2560]{1,0:T(8,128)(2,1)S(1)}, u32[]{:S(2)}, u32[]{:S(2)}) %collective-permute-start.17) | collective-permute-done | bytes 655392 | tf_op jit(solution)/shard_map/ppermute | solution.py:47
  101.8 1.6 collective-permute-start.19
  103.9 1.2 fusion.51
  105.1 1.6 collective-permute-start.26
  106.7 1.0 collective-permute-start.25
  108.4 1.3 fusion.21
  109.7 9.8 %collective-permute-done.19 = bf16[2,64,2560]{2,1,0:T(8,128)(2,1)S(1)} collective-permute-done((bf16[2,64,2560]{2,1,0:T(8,128)(2,1)S(1)}, bf16[2,64,2560]{2,1,0:T(8,128)(2,1)S(1)}, u32[]{:S(2)}, u32[]{:S(2)}) %collective-permute-start.19) | collective-permute-done | bytes 655392 | tf_op jit(solution)/shard_map/ppermute | solution.py:47
  119.5 1.3 collective-permute-start.23
  120.8 11.0 %collective-permute-done.20 = bf16[2,64,2560]{2,1,0:T(8,128)(2,1)S(1)} collective-permute-done((bf16[2,64,2560]{2,1,0:T(8,128)(2,1)S(1)}, bf16[2,64,2560]{2,1,0:T(8,128)(2,1)S(1)}, u32[]{:S(2)}, u32[]{:S(2)}) %collective-permute-start.20) | collective-permute-done | bytes 655392 | tf_op jit(solution)/shard_map/ppermute | solution.py:47
  132.1 1.7 %collective-permute-start.21 = (bf16[2,64,2560]{2,1,0:T(8,128)(2,1)S(1)}, bf16[2,64,2560]{2,1,0:T(8,128)(2,1)S(1)}, u32[]{:S(2)}, u32[]{:S(2)}) collective-permute-start(bf16[2,64,2560]{2,1,0:T(8,128)(2,1)S(1)} %get-tuple-element.159), channel_id=1, source_target_pairs={{0,8},{8,0},{16,24},{24,16},{1,9},{9,1},{17,25},{25,17},{2,10},{10... | collective-permute-start | bytes 1966088 | tf_op jit(solution)/shard_map/ppermute | solution.py:47
  133.8 1.2 fusion.18.refs_0_
  135.1 12.5 %collective-permute-done.21 = bf16[2,64,2560]{2,1,0:T(8,128)(2,1)S(1)} collective-permute-done((bf16[2,64,2560]{2,1,0:T(8,128)(2,1)S(1)}, bf16[2,64,2560]{2,1,0:T(8,128)(2,1)S(1)}, u32[]{:S(2)}, u32[]{:S(2)}) %collective-permute-start.21) | collective-permute-done | bytes 655392 | tf_op jit(solution)/shard_map/ppermute | solution.py:47
  147.8 1.5 collective-permute-start.22
  149.3 5.7 %shard_map.88 = (bf16[256,3200]{1,0:T(8,128)(2,1)}, bf16[256,3200]{1,0:T(8,128)(2,1)}) custom-call(s32[4]{0:T(128)S(1)} %pad_add_fusion.place, bf16[256,3200]{1,0:T(8,128)(2,1)S(1)} %copy-done, bf16[256,3200]{1,0:T(8,128)(2,1)S(1)} %copy-done.2, bf16[800,256]{1,0:T(8,128)(2,1)S(1)} %fusion.18.refs_0_, bf16[800,256]{1,0:T(8,128)(2,1)S(1)} %collective-permute-done.23.refs_1_, ...), custom_call_target="tpu_custom_call" | custom-call | flops 19660800 | bytes 8192000 | tf_op jit(solution)/shard_map/pallas_call | solution.py:52
  155.0 3.3 %convert_add_fusion.1 = f32[400,2560]{1,0:T(8,128)} fusion(bf16[272,2560]{1,0:T(8,128)(2,1)S(1)} %collective-permute-done.26, bf16[128,2560]{1,0:T(8,128)(2,1)S(1)} %collective-permute-done.17, f32[400,2560]{1,0:T(8,128)S(1)} %fusion.51, bf16[400,512]{1,0:T(8,128)(2,1)S(1)} %get-tuple-element.155, bf16[512,2560]{1,0:T(8,128)(2,1)S(1)} %bitcast.84), kind=kOutput, calls=%fused_computation.7 | convolution fusion | flops 1055744000 | bytes 13271040 | tf_op jit(solution)/shard_map/dot_general | solution.py:166
  158.3 5.1 %collective-permute-done.22 = bf16[64,2560]{1,0:T(8,128)(2,1)S(1)} collective-permute-done((bf16[64,2560]{1,0:T(8,128)(2,1)S(1)}, bf16[64,2560]{1,0:T(8,128)(2,1)S(1)}, u32[]{:S(2)}, u32[]{:S(2)}) %collective-permute-start.22) | collective-permute-done | bytes 327712 | tf_op jit(solution)/shard_map/ppermute | solution.py:47
  163.3 0.8 fusion.43
  (52 shorter events, 8.1 us)
Async XLA Ops:
  0.6 9.4 %copy-start = (bf16[256,3200]{1,0:T(8,128)(2,1)S(1)}, bf16[256,3200]{1,0:T(8,128)(2,1)}, u32[]{:S(2)}) copy-start(bf16[256,3200]{1,0:T(8,128)(2,1)} %gate.3) | copy-start | bytes 4915204
  0.6 19.0 %collective-permute-start = (bf16[64,2560]{1,0:T(8,128)(2,1)}, bf16[64,2560]{1,0:T(8,128)(2,1)S(1)}, u32[]{:S(2)}, u32[]{:S(2)}) collective-permute-start(bf16[64,2560]{1,0:T(8,128)(2,1)} %param.9), channel_id=1, source_target_pairs={{0,16},{8,24},{16,0},{24,8},{1,17},{9,25},{17,1},{25,9},{2,18},{10... | collective-permute-start | bytes 983048 | tf_op jit(solution)/shard_map/ppermute | solution.py:47
  5.7 1.6 copy-start.3
  7.3 12.4 %copy-start.4 = (bf16[64,2560]{1,0:T(8,128)(2,1)S(1)}, bf16[64,2560]{1,0:T(8,128)(2,1)}, u32[]{:S(2)}) copy-start(bf16[64,2560]{1,0:T(8,128)(2,1)} %param.9) | copy-start | bytes 983044
  8.4 38.6 %collective-permute-start.5 = (bf16[400,1280]{1,0:T(8,128)(2,1)S(1)}, bf16[400,1280]{1,0:T(8,128)(2,1)S(1)}, u32[]{:S(2)}, u32[]{:S(2)}) collective-permute-start(bf16[400,1280]{1,0:T(8,128)(2,1)S(1)} %get-tuple-element.81.own_a), channel_id=1, source_target_pairs={{0,4},{4,0},{1,5},{5,1},{2,6},{6,2},{3,7},{7,3},{8,12},{12,8},{9,1... | collective-permute-start | bytes 3072008 | tf_op jit(solution)/shard_map/ppermute | solution.py:47
  10.0 1.4 copy-start.1
  19.8 27.3 %collective-permute-start.1 = (bf16[2,64,2560]{2,1,0:T(8,128)(2,1)S(1)}, bf16[2,64,2560]{2,1,0:T(8,128)(2,1)S(1)}, u32[]{:S(2)}, u32[]{:S(2)}) collective-permute-start(bf16[2,64,2560]{2,1,0:T(8,128)(2,1)S(1)} %pad_maximum_fusion.2), channel_id=1, source_target_pairs={{0,8},{8,0},{16,24},{24,16},{1,9},{9,1},{17,25},{25,17},{2,10},{10... | collective-permute-start | bytes 1966088 | tf_op jit(solution)/shard_map/ppermute | solution.py:47
  20.6 26.4 %collective-permute-start.2 = (bf16[2,64,2560]{2,1,0:T(8,128)(2,1)S(1)}, bf16[2,64,2560]{2,1,0:T(8,128)(2,1)S(1)}, u32[]{:S(2)}, u32[]{:S(2)}) collective-permute-start(bf16[2,64,2560]{2,1,0:T(8,128)(2,1)S(1)} %pad_maximum_fusion.2), channel_id=1, source_target_pairs={{0,2},{2,0},{1,3},{3,1},{4,6},{6,4},{5,7},{7,5},{8,10},{10,8},{9,1... | collective-permute-start | bytes 1966088 | tf_op jit(solution)/shard_map/ppermute | solution.py:47
  22.2 18.0 %collective-permute-start.3 = (bf16[400,256]{1,0:T(8,128)(2,1)S(1)}, bf16[400,256]{1,0:T(8,128)(2,1)S(1)}, u32[]{:S(2)}, u32[]{:S(2)}) collective-permute-start(bf16[400,256]{1,0:T(8,128)(2,1)S(1)} %get-tuple-element.90), channel_id=1, source_target_pairs={{0,16},{8,24},{16,0},{24,8},{1,17},{9,25},{17,1},{25,9},{2,18},{10... | collective-permute-start | bytes 614408 | tf_op jit(solution)/shard_map/ppermute | solution.py:47
  25.4 21.6 %collective-permute-start.4 = (bf16[400,256]{1,0:T(8,128)(2,1)S(1)}, bf16[400,256]{1,0:T(8,128)(2,1)S(1)}, u32[]{:S(2)}, u32[]{:S(2)}) collective-permute-start(bf16[400,256]{1,0:T(8,128)(2,1)S(1)} %get-tuple-element.91), channel_id=1, source_target_pairs={{0,24},{8,16},{16,8},{24,0},{1,25},{9,17},{17,9},{25,1},{2,26},{10... | collective-permute-start | bytes 614408 | tf_op jit(solution)/shard_map/ppermute | solution.py:47
  47.1 24.1 %collective-permute-start.10 = (bf16[400,1280]{1,0:T(8,128)(2,1)S(1)}, bf16[400,1280]{1,0:T(8,128)(2,1)S(1)}, u32[]{:S(2)}, u32[]{:S(2)}) collective-permute-start(bf16[400,1280]{1,0:T(8,128)(2,1)S(1)} %get-tuple-element.96.own_b), channel_id=1, source_target_pairs={{0,4},{4,0},{1,5},{5,1},{2,6},{6,2},{3,7},{7,3},{8,12},{12,8},{9,1... | collective-permute-start | bytes 3072008 | tf_op jit(solution)/shard_map/ppermute | solution.py:47
  48.6 20.6 %collective-permute-start.6 = (bf16[2,64,2560]{2,1,0:T(8,128)(2,1)S(1)}, bf16[2,64,2560]{2,1,0:T(8,128)(2,1)S(1)}, u32[]{:S(2)}, u32[]{:S(2)}) collective-permute-start(bf16[2,64,2560]{2,1,0:T(8,128)(2,1)S(1)} %collective-permute-done.1), channel_id=1, source_target_pairs={{0,2},{2,0},{1,3},{3,1},{4,6},{6,4},{5,7},{7,5},{8,10},{10,8},{9,1... | collective-permute-start | bytes 1966088 | tf_op jit(solution)/shard_map/ppermute | solution.py:47
  50.1 19.1 %collective-permute-start.7 = (bf16[800,256]{1,0:T(8,128)(2,1)S(1)}, bf16[800,256]{1,0:T(8,128)(2,1)S(1)}, u32[]{:S(2)}, u32[]{:S(2)}) collective-permute-start(bf16[800,256]{1,0:T(8,128)(2,1)S(1)} %get-tuple-element.100), channel_id=1, source_target_pairs={{0,8},{8,0},{16,24},{24,16},{1,9},{9,1},{17,25},{25,17},{2,10},{10... | collective-permute-start | bytes 1228808 | tf_op jit(solution)/shard_map/ppermute | solution.py:47
  50.1 14.4 %collective-permute-start.8 = (bf16[400,256]{1,0:T(8,128)(2,1)S(1)}, bf16[400,256]{1,0:T(8,128)(2,1)S(1)}, u32[]{:S(2)}, u32[]{:S(2)}) collective-permute-start(bf16[400,256]{1,0:T(8,128)(2,1)S(1)} %get-tuple-element.103), channel_id=1, source_target_pairs={{0,16},{8,24},{16,0},{24,8},{1,17},{9,25},{17,1},{25,9},{2,18},{10... | collective-permute-start | bytes 614408 | tf_op jit(solution)/shard_map/ppermute | solution.py:47
  52.4 15.8 %collective-permute-start.9 = (bf16[400,256]{1,0:T(8,128)(2,1)S(1)}, bf16[400,256]{1,0:T(8,128)(2,1)S(1)}, u32[]{:S(2)}, u32[]{:S(2)}) collective-permute-start(bf16[400,256]{1,0:T(8,128)(2,1)S(1)} %get-tuple-element.104), channel_id=1, source_target_pairs={{0,24},{8,16},{16,8},{24,0},{1,25},{9,17},{17,9},{25,1},{2,26},{10... | collective-permute-start | bytes 614408 | tf_op jit(solution)/shard_map/ppermute | solution.py:47
  64.5 8.8 %collective-permute-start.11 = (bf16[2,64,2560]{2,1,0:T(8,128)(2,1)S(1)}, bf16[2,64,2560]{2,1,0:T(8,128)(2,1)S(1)}, u32[]{:S(2)}, u32[]{:S(2)}) collective-permute-start(bf16[2,64,2560]{2,1,0:T(8,128)(2,1)S(1)} %pad_maximum_fusion.2), channel_id=1, source_target_pairs={{0,1},{1,0},{2,3},{3,2},{4,5},{5,4},{6,7},{7,6},{8,9},{9,8},{10,11... | collective-permute-start | bytes 1966088 | tf_op jit(solution)/shard_map/ppermute | solution.py:47
  68.2 5.1 %collective-permute-start.13 = (bf16[2,64,2560]{2,1,0:T(8,128)(2,1)S(1)}, bf16[2,64,2560]{2,1,0:T(8,128)(2,1)S(1)}, u32[]{:S(2)}, u32[]{:S(2)}) collective-permute-start(bf16[2,64,2560]{2,1,0:T(8,128)(2,1)S(1)} %collective-permute-done.1), channel_id=1, source_target_pairs={{0,1},{1,0},{2,3},{3,2},{4,5},{5,4},{6,7},{7,6},{8,9},{9,8},{10,11... | collective-permute-start | bytes 1966088 | tf_op jit(solution)/shard_map/ppermute | solution.py:47
  69.2 4.1 %collective-permute-start.12 = (bf16[2,64,2560]{2,1,0:T(8,128)(2,1)S(1)}, bf16[2,64,2560]{2,1,0:T(8,128)(2,1)S(1)}, u32[]{:S(2)}, u32[]{:S(2)}) collective-permute-start(bf16[2,64,2560]{2,1,0:T(8,128)(2,1)S(1)} %collective-permute-done.2), channel_id=1, source_target_pairs={{0,1},{1,0},{2,3},{3,2},{4,5},{5,4},{6,7},{7,6},{8,9},{9,8},{10,11... | collective-permute-start | bytes 1966088 | tf_op jit(solution)/shard_map/ppermute | solution.py:47
  71.2 2.2 %collective-permute-start.14 = (bf16[2,64,2560]{2,1,0:T(8,128)(2,1)S(1)}, bf16[2,64,2560]{2,1,0:T(8,128)(2,1)S(1)}, u32[]{:S(2)}, u32[]{:S(2)}) collective-permute-start(bf16[2,64,2560]{2,1,0:T(8,128)(2,1)S(1)} %collective-permute-done.6), channel_id=1, source_target_pairs={{0,1},{1,0},{2,3},{3,2},{4,5},{5,4},{6,7},{7,6},{8,9},{9,8},{10,11... | collective-permute-start | bytes 1966088 | tf_op jit(solution)/shard_map/ppermute | solution.py:47
  83.4 7.8 %collective-permute-start.18 = (bf16[512,2560]{1,0:T(8,128)(2,1)S(1)}, bf16[512,2560]{1,0:T(8,128)(2,1)S(1)}, u32[]{:S(2)}, u32[]{:S(2)}) collective-permute-start(bf16[512,2560]{1,0:T(8,128)(2,1)S(1)} %convolution_convert_fusion), channel_id=1, source_target_pairs={{0,1},{1,0},{2,3},{3,2},{4,5},{5,4},{6,7},{7,6},{8,9},{9,8},{10,11... | collective-permute-start | bytes 7864328 | tf_op jit(solution)/shard_map/ppermute | solution.py:47
  83.9 16.7 %collective-permute-start.17 = (bf16[128,2560]{1,0:T(8,128)(2,1)S(1)}, bf16[128,2560]{1,0:T(8,128)(2,1)S(1)}, u32[]{:S(2)}, u32[]{:S(2)}) collective-permute-start(bf16[128,2560]{1,0:T(8,128)(2,1)S(1)} %fusion.4), channel_id=1, source_target_pairs={{0,4},{4,0},{1,5},{5,1},{2,6},{6,2},{3,7},{7,3},{8,12},{12,8},{9,1... | collective-permute-start | bytes 1966088 | tf_op jit(solution)/shard_map/ppermute | solution.py:47
  85.4 11.6 %collective-permute-start.15 = (bf16[256,256]{1,0:T(8,128)(2,1)S(1)}, bf16[256,256]{1,0:T(8,128)(2,1)S(1)}, u32[]{:S(2)}, u32[]{:S(2)}) collective-permute-start(bf16[256,256]{1,0:T(8,128)(2,1)S(1)} %fusion.34), channel_id=1, source_target_pairs={{0,16},{8,24},{16,0},{24,8},{1,17},{9,25},{17,1},{25,9},{2,18},{10... | collective-permute-start | bytes 393224 | tf_op jit(solution)/shard_map/ppermute | solution.py:47
  85.5 11.5 %collective-permute-start.16 = (bf16[256,256]{1,0:T(8,128)(2,1)S(1)}, bf16[256,256]{1,0:T(8,128)(2,1)S(1)}, u32[]{:S(2)}, u32[]{:S(2)}) collective-permute-start(bf16[256,256]{1,0:T(8,128)(2,1)S(1)} %fusion.37), channel_id=1, source_target_pairs={{0,24},{8,16},{16,8},{24,0},{1,25},{9,17},{17,9},{25,1},{2,26},{10... | collective-permute-start | bytes 393224 | tf_op jit(solution)/shard_map/ppermute | solution.py:47
  101.8 17.7 %collective-permute-start.19 = (bf16[2,64,2560]{2,1,0:T(8,128)(2,1)S(1)}, bf16[2,64,2560]{2,1,0:T(8,128)(2,1)S(1)}, u32[]{:S(2)}, u32[]{:S(2)}) collective-permute-start(bf16[2,64,2560]{2,1,0:T(8,128)(2,1)S(1)} %get-tuple-element.160), channel_id=1, source_target_pairs={{0,2},{2,0},{1,3},{3,1},{4,6},{6,4},{5,7},{7,5},{8,10},{10,8},{9,1... | collective-permute-start | bytes 1966088 | tf_op jit(solution)/shard_map/ppermute | solution.py:47
  103.4 28.4 %collective-permute-start.20 = (bf16[2,64,2560]{2,1,0:T(8,128)(2,1)S(1)}, bf16[2,64,2560]{2,1,0:T(8,128)(2,1)S(1)}, u32[]{:S(2)}, u32[]{:S(2)}) collective-permute-start(bf16[2,64,2560]{2,1,0:T(8,128)(2,1)S(1)} %get-tuple-element.161), channel_id=1, source_target_pairs={{0,2},{2,0},{1,3},{3,1},{4,6},{6,4},{5,7},{7,5},{8,10},{10,8},{9,1... | collective-permute-start | bytes 1966088 | tf_op jit(solution)/shard_map/ppermute | solution.py:47
  105.1 49.9 %collective-permute-start.26 = (bf16[272,2560]{1,0:T(8,128)(2,1)S(1)}, bf16[272,2560]{1,0:T(8,128)(2,1)S(1)}, u32[]{:S(2)}, u32[]{:S(2)}) collective-permute-start(bf16[272,2560]{1,0:T(8,128)(2,1)S(1)} %fusion.2), channel_id=1, source_target_pairs={{0,4},{4,0},{1,5},{5,1},{2,6},{6,2},{3,7},{7,3},{8,12},{12,8},{9,1... | collective-permute-start | bytes 4177928 | tf_op jit(solution)/shard_map/ppermute | solution.py:47
  106.7 28.4 %collective-permute-start.25 = (bf16[544,256]{1,0:T(8,128)(2,1)S(1)}, bf16[544,256]{1,0:T(8,128)(2,1)S(1)}, u32[]{:S(2)}, u32[]{:S(2)}) collective-permute-start(bf16[544,256]{1,0:T(8,128)(2,1)S(1)} %fusion.27), channel_id=1, source_target_pairs={{0,24},{8,16},{16,8},{24,0},{1,25},{9,17},{17,9},{25,1},{2,26},{10... | collective-permute-start | bytes 835592 | tf_op jit(solution)/shard_map/ppermute | solution.py:47
  107.7 27.4 %collective-permute-start.24 = (bf16[544,256]{1,0:T(8,128)(2,1)S(1)}, bf16[544,256]{1,0:T(8,128)(2,1)S(1)}, u32[]{:S(2)}, u32[]{:S(2)}) collective-permute-start(bf16[544,256]{1,0:T(8,128)(2,1)S(1)} %fusion.24), channel_id=1, source_target_pairs={{0,16},{8,24},{16,0},{24,8},{1,17},{9,25},{17,1},{25,9},{2,18},{10... | collective-permute-start | bytes 835592 | tf_op jit(solution)/shard_map/ppermute | solution.py:47
  119.5 29.8 %collective-permute-start.23 = (bf16[800,256]{1,0:T(8,128)(2,1)S(1)}, bf16[800,256]{1,0:T(8,128)(2,1)S(1)}, u32[]{:S(2)}, u32[]{:S(2)}) collective-permute-start(bf16[800,256]{1,0:T(8,128)(2,1)S(1)} %fusion.21), channel_id=1, source_target_pairs={{0,8},{8,0},{16,24},{24,16},{1,9},{9,1},{17,25},{25,17},{2,10},{10... | collective-permute-start | bytes 1228808 | tf_op jit(solution)/shard_map/ppermute | solution.py:47
  132.1 15.5 %collective-permute-start.21 = (bf16[2,64,2560]{2,1,0:T(8,128)(2,1)S(1)}, bf16[2,64,2560]{2,1,0:T(8,128)(2,1)S(1)}, u32[]{:S(2)}, u32[]{:S(2)}) collective-permute-start(bf16[2,64,2560]{2,1,0:T(8,128)(2,1)S(1)} %get-tuple-element.159), channel_id=1, source_target_pairs={{0,8},{8,0},{16,24},{24,16},{1,9},{9,1},{17,25},{25,17},{2,10},{10... | collective-permute-start | bytes 1966088 | tf_op jit(solution)/shard_map/ppermute | solution.py:47
  135.0 14.3 %copy-start.2 = (bf16[256,3200]{1,0:T(8,128)(2,1)S(1)}, bf16[256,3200]{1,0:T(8,128)(2,1)}, u32[]{:S(2)}) copy-start(bf16[256,3200]{1,0:T(8,128)(2,1)} %up.3) | copy-start | bytes 4915204
  147.8 15.5 %collective-permute-start.22 = (bf16[64,2560]{1,0:T(8,128)(2,1)S(1)}, bf16[64,2560]{1,0:T(8,128)(2,1)S(1)}, u32[]{:S(2)}, u32[]{:S(2)}) collective-permute-start(bf16[64,2560]{1,0:T(8,128)(2,1)S(1)} %fusion.44), channel_id=1, source_target_pairs={{0,16},{8,24},{16,0},{24,8},{1,17},{9,25},{17,1},{25,9},{2,18},{10... | collective-permute-start | bytes 983048 | tf_op jit(solution)/shard_map/ppermute | solution.py:47
